TPU v7x, 128 devices: a whole 4x4x4 slice. The times are simulated.
128 devices in a mesh: lon: 32 (over z, x, y_hi), lat: 4 (over y_lo, core).
Axes of the slice: x: 4, y: 4 (y_hi: 2, y_lo: 2; y = y_hi * 2 + y_lo), z: 4, core: 2. Of those that a mesh axis runs over, the one named last changes fastest.
Arguments:
- field_in: bfloat16 [384, 1792, 128], P('lat', 'lon'), may hold values from -6 to 6
- conv_out: bfloat16 [384, 1792, 128], P('lat', 'lon'), may hold values from -6 to 6
- cotangent: bfloat16 [384, 1792, 128], P('lat', 'lon'), may hold values from -6 to 6
- kernel: float32 [49, 128], replicated, may hold values from -0.875 to 0.875
- ln_gain: float32 [128], replicated, may hold values from 0.5 to 1.5
- ln_bias: float32 [128], replicated, may hold values from -3 to 3
- w_in: bfloat16 [128, 512], replicated, may hold values from -0.5 to 0.5
- b_in: float32 [512], replicated, may hold values from -3 to 3
- w_out: bfloat16 [512, 128], replicated, may hold values from -0.25 to 0.25
- b_out: float32 [128], replicated, may hold values from -3 to 3
- layer_scale: float32 [128], replicated, may hold values from 0.5 to 1.5
Outputs:
- d_field: bfloat16 [384, 1792, 128], P('lat', 'lon')
- d_kernel: float32 [49, 128], replicated
- d_conv_bias: float32 [128], replicated
- d_ln_gain: float32 [128], replicated
- d_ln_bias: float32 [128], replicated
- d_w_in: float32 [128, 512], replicated
- d_b_in: float32 [512], replicated
- d_w_out: float32 [512, 128], replicated
- d_b_out: float32 [128], replicated
- d_layer_scale: float32 [128], replicated
- grad_norm: float32 [], replicated
All inputs are finite; a program needn't handle non-finite values.
Results may differ from a plain program's by a relative error of at most 0.0075.
Values may be sent and summed in bfloat16 or wider, within the bound.
A program may use at most 64 MiB of HBM per device.

v0:
```python
import math

import jax
import jax.numpy as jnp
from jax import lax
from jax.sharding import PartitionSpec as P

norm_eps = 1e-06
gelu_coef = 0.044715
gelu_root = math.sqrt(2.0 / math.pi)


def extended(shard, sides, width):
    for axis, dim in sides:
        size, length = (lax.axis_size(axis), shard.shape[dim])
        up = [(i, (i + 1) % size) for i in range(size)]
        down = [(j, i) for i, j in up]
        last = lax.slice_in_dim(shard, length - width, length, axis=dim)
        leading = lax.slice_in_dim(shard, 0, width, axis=dim)
        before = lax.ppermute(last, axis, up)
        after = lax.ppermute(leading, axis, down)
        shard = jnp.concatenate([before, shard, after], axis=dim)
    return shard


def latitude_weight(row_ids, total_rows):
    place = (row_ids.astype(jnp.float32) + 0.5) / jnp.float32(total_rows) - 0.5
    return jnp.cos(jnp.float32(math.pi) * place)


def gelu_parts(pre):
    inner = gelu_root * (pre + gelu_coef * pre * pre * pre)
    tangent = jnp.tanh(inner)
    value = 0.5 * pre * (1.0 + tangent)
    slope = 0.5 * (1.0 + tangent) + 0.5 * pre * (1.0 - tangent * tangent) * gelu_root * (
        1.0 + 3.0 * gelu_coef * pre * pre
    )
    return (value, slope)


def contract_rows(left, right):
    return lax.dot_general(
        left, right, (((0,), (0,)), ((), ())), preferred_element_type=jnp.float32
    )


def contract_last(left, right):
    return lax.dot_general(
        left, right, (((1,), (1,)), ((), ())), preferred_element_type=jnp.float32
    )


def channel_backward(conv_rows, dy_rows, ln_gain, ln_bias, w_in, b_in, w_out, b_out, layer_scale):
    values = conv_rows.astype(jnp.float32)
    center = values - jnp.mean(values, -1, keepdims=True)
    rstd = lax.rsqrt(jnp.mean(center * center, -1, keepdims=True) + norm_eps)
    normed = center * rstd
    zed = (normed * ln_gain + ln_bias).astype(jnp.bfloat16)
    pre = jnp.dot(zed, w_in, preferred_element_type=jnp.float32) + b_in
    act_value, slope = gelu_parts(pre)
    act = act_value.astype(jnp.bfloat16)
    out = jnp.dot(act, w_out, preferred_element_type=jnp.float32) + b_out
    dy_values = dy_rows.astype(jnp.float32)
    g_scale = jnp.sum(dy_values * out, 0)
    d_out = (layer_scale * dy_values).astype(jnp.bfloat16)
    g_b_out = jnp.sum(d_out.astype(jnp.float32), 0)
    g_w_out = contract_rows(act, d_out)
    d_act = contract_last(d_out, w_out)
    d_pre = (d_act * slope).astype(jnp.bfloat16)
    g_b_in = jnp.sum(d_pre.astype(jnp.float32), 0)
    g_w_in = contract_rows(zed, d_pre)
    d_zed = contract_last(d_pre, w_in)
    g_ln_gain = jnp.sum(d_zed * normed, 0)
    g_ln_bias = jnp.sum(d_zed, 0)
    d_norm = d_zed * ln_gain
    du_value = rstd * (
        d_norm
        - jnp.mean(d_norm, -1, keepdims=True)
        - normed * jnp.mean(d_norm * normed, -1, keepdims=True)
    )
    du_rows = du_value.astype(jnp.bfloat16)
    g_conv_bias = jnp.sum(du_rows.astype(jnp.float32), 0)
    return (du_rows, (g_conv_bias, g_ln_gain, g_ln_bias, g_w_in, g_b_in, g_w_out, g_b_out, g_scale))


def polar_zero(padded, row_dim, rows):
    band = lax.axis_index("lat")
    last_band = lax.axis_size("lat") - 1
    position = jnp.arange(rows + 6, dtype=jnp.int32)
    outside = (position < 3) & (band == 0) | (position >= rows + 3) & (band == last_band)
    shape = [1] * padded.ndim
    shape[row_dim] = rows + 6
    keep = jnp.logical_not(outside).reshape(shape)
    return jnp.where(keep, padded, jnp.zeros((), padded.dtype))


def on_device(
    field_in, conv_out, cotangent, kernel, ln_gain, ln_bias, w_in, b_in, w_out, b_out, layer_scale
):
    rows, cols, width = conv_out.shape
    du_flat, parts = channel_backward(
        conv_out.reshape(rows * cols, width),
        cotangent.reshape(rows * cols, width),
        ln_gain,
        ln_bias,
        w_in,
        b_in,
        w_out,
        b_out,
        layer_scale,
    )
    du_local = du_flat.reshape(rows, cols, width)
    total_rows = rows * lax.axis_size("lat")
    total_cols = cols * lax.axis_size("lon")
    first_row = lax.axis_index("lat") * rows
    row_cos = latitude_weight(first_row + jnp.arange(rows, dtype=jnp.int32), total_rows)
    kernel_terms = []
    stacked = jnp.stack([field_in, du_local], 0)
    padded = extended(stacked, (("lon", 2), ("lat", 1)), 3)
    padded = polar_zero(padded, 1, rows)
    du_pad = padded[1].astype(jnp.float32)
    pad_cos = latitude_weight(first_row - 3 + jnp.arange(rows + 6, dtype=jnp.int32), total_rows)
    weighted = pad_cos[:, None, None] * padded[0].astype(jnp.float32)
    inner = du_local.astype(jnp.float32)
    for lat_off in range(-3, 4):
        for lon_off in range(-3, 4):
            kernel_terms.append(
                jnp.sum(
                    inner
                    * weighted[3 + lat_off : 3 + lat_off + rows, 3 + lon_off : 3 + lon_off + cols],
                    (0, 1),
                )
            )
    conv_sum = jnp.zeros((rows, cols, width), jnp.float32)
    for lat_off in range(-3, 4):
        for lon_off in range(-3, 4):
            tap = (lat_off + 3) * 7 + lon_off + 3
            conv_sum = (
                conv_sum
                + kernel[tap]
                * du_pad[3 - lat_off : 3 - lat_off + rows, 3 - lon_off : 3 - lon_off + cols]
            )
    d_field = (cotangent.astype(jnp.float32) + row_cos[:, None, None] * conv_sum).astype(
        jnp.bfloat16
    )
    locals_all = (jnp.stack(kernel_terms),) + parts
    factor = jnp.float32(float(total_rows * total_cols) ** (-0.5))
    totals = lax.psum(locals_all, ("lon", "lat"))
    scaled = tuple((total * factor for total in totals))
    grad_norm = jnp.sqrt(sum((jnp.sum(part * part) for part in scaled)))
    d_kernel, d_conv_bias, d_ln_gain, d_ln_bias, d_w_in, d_b_in, d_w_out, d_b_out, d_layer_scale = (
        scaled
    )
    return (
        d_field,
        d_kernel,
        d_conv_bias,
        d_ln_gain,
        d_ln_bias,
        d_w_in,
        d_b_in,
        d_w_out,
        d_b_out,
        d_layer_scale,
        grad_norm,
    )


def solution(mesh):
    return jax.shard_map(
        on_device,
        mesh=mesh,
        in_specs=(
            P("lat", "lon", None),
            P("lat", "lon", None),
            P("lat", "lon", None),
            P(),
            P(),
            P(),
            P(),
            P(),
            P(),
            P(),
            P(),
        ),
        out_specs=(P("lat", "lon", None), P(), P(), P(), P(), P(), P(), P(), P(), P(), P()),
        check_vma=False,
    )
```

profile of v0, /device:TPU:1, one launch (start us, length us, event | category | flops | bytes accessed | tf_op | source)
XLA Modules:
  0.0 209.2 jit_solution(2613200669813708041)
XLA Ops:
  7.2 0.0 copy-start
  7.2 0.0 copy-start.1
  7.2 0.0 copy-start.4
  7.2 0.0 copy-start.9
  7.2 0.0 copy-start.8
  7.2 0.0 copy-start.10
  7.2 0.0 all-reduce.4.cloned.1.call-start
  7.3 2.3 %convert_reduce_fusion.2 = f32[96,56]{1,0:T(8,128)S(1)} fusion(bf16[96,56,128]{2,1,0:T(8,128)(2,1)} %param.12), kind=kLoop, calls=%fused_computation.225 | loop fusion | flops 1370880 | bytes 1397760 | tf_op jit(solution)/shard_map/reduce_sum | solution.py:55
  9.6 2.7 %multiply_reduce_fusion.2 = f32[96,56]{1,0:T(8,128)S(1)} fusion(bf16[96,56,128]{2,1,0:T(8,128)(2,1)} %param.12, f32[96,56]{1,0:T(8,128)S(1)} %broadcast_multiply_fusion.2), kind=kLoop, calls=%fused_computation.223 | loop fusion | flops 2747136 | bytes 1419264 | tf_op jit(solution)/shard_map/reduce_sum | solution.py:56
  12.3 0.1 div.30
  12.4 0.1 rsqrt.12
  12.5 0.0 copy-done.4
  12.5 0.0 copy-done.9
  12.5 0.0 copy-start.12
  12.5 0.3 fusion.109
  12.8 0.0 copy-done.1
  12.8 0.0 copy-done.8
  12.8 0.0 copy-done.10
  12.9 3.0 %add_convert_fusion = bf16[5376,128]{1,0:T(8,128)(2,1)S(1)} fusion(bf16[96,56,128]{2,1,0:T(8,128)(2,1)S(1)} %copy-done.1, f32[128]{0:T(128)S(1)} %copy-done.10, f32[128]{0:T(128)S(1)} %copy-done.8, f32[5376]{0:T(1024)S(1)} %div.30, f32[5376]{0:T(1024)S(1)} %rsqrt.12), kind=kLoop, calls=%fused_computation.222 | loop fusion | flops 4128768 | bytes 2796544 | tf_op jit(solution)/shard_map/convert_element_type | solution.py:58
  15.9 0.0 copy-start.11
  15.9 4.2 %multiply_convert_fusion = (bf16[5376,512]{1,0:T(8,128)(2,1)S(1)}, f32[5376,512]{1,0:T(8,128)S(1)}) fusion(f32[512]{0:T(512)S(1)} %copy-done.12, bf16[5376,128]{1,0:T(8,128)(2,1)S(1)} %add_convert_fusion, bf16[128,512]{1,0:T(8,128)(2,1)S(1)} %copy-done), kind=kOutput, calls=%fused_computation.9 | convolution fusion | flops 732168192 | bytes 18024448 | tf_op jit(solution)/shard_map/dot_general | solution.py:59
  20.1 9.1 %convert_reduce_fusion = (f32[512]{0:T(512)}, bf16[5376,512]{1,0:T(8,128)(2,1)S(1)}) fusion(f32[5376,512]{1,0:T(8,128)S(1)} %get-tuple-element.151, f32[512]{0:T(512)S(1)} %copy-done.12, bf16[5376,128]{1,0:T(8,128)(2,1)S(1)} %fusion.109, bf16[512,128]{1,0:T(8,128)(2,1)S(1)} %copy-done.11), kind=kOutput, calls=%fused_computation.10 | convolution fusion | flops 765197824 | bytes 18026496 | tf_op jit(solution)/shard_map/dot_general | solution.py:48
  29.2 3.0 %multiply_reduce_fusion = (f32[128]{0:T(128)}, f32[5376]{0:T(1024)S(1)}, f32[5376]{0:T(1024)S(1)}, f32[128]{0:T(128)}, f32[5376,128]{1,0:T(8,128)S(1)}) fusion(bf16[96,56,128]{2,1,0:T(8,128)(2,1)S(1)} %copy-done.1, f32[5376]{0:T(1024)S(1)} %div.30, f32[5376]{0:T(1024)S(1)} %rsqrt.12, f32[128]{0:T(128)S(1)} %copy-done.8, ...), kind=kOutput, calls=%fused_computation.219 | convolution fusion | flops 711513344 | bytes 9852416 | tf_op jit(solution)/shard_map/dot_general | solution.py:48
  32.2 0.0 copy-start.2
  32.2 4.0 %convert_reduce_fusion.3 = (f32[128]{0:T(128)S(1)}, bf16[5376,128]{1,0:T(8,128)(2,1)S(1)}) fusion(f32[5376]{0:T(1024)S(1)} %get-tuple-element.152, f32[5376]{0:T(1024)S(1)} %div.30, bf16[96,56,128]{2,1,0:T(8,128)(2,1)S(1)} %copy-done.1, f32[5376]{0:T(1024)S(1)} %get-tuple-element.153, f32[5376,128]{1,0:T(8,128)S(1)} %get-tuple-element.147, ...), kind=kLoop, calls=%fused_computation.230 | loop fusion | flops 7569280 | bytes 5592064 | tf_op jit(solution)/shard_map/reduce_sum | solution.py:82
  36.2 0.8 pad_maximum_fusion.1
  37.0 3.7 %collective-permute-start = (bf16[2,96,3,128]{3,2,1,0:T(4,128)(2,1)}, bf16[2,96,3,128]{3,2,1,0:T(4,128)(2,1)S(1)}, u32[]{:S(2)}, u32[]{:S(2)}) collective-permute-start(bf16[2,96,3,128]{3,2,1,0:T(4,128)(2,1)} %get-tuple-element.96), channel_id=1, source_target_pairs={{0,4},{4,8},{8,12},{12,16},{16,20},{20,24},{24,28},{28,32},{32,36}... | collective-permute-start | bytes 442376 | tf_op jit(solution)/shard_map/ppermute | solution.py:20
  40.8 5.7 %collective-permute-start.1 = (bf16[2,96,3,128]{3,2,1,0:T(4,128)(2,1)S(1)}, bf16[2,96,3,128]{3,2,1,0:T(4,128)(2,1)S(1)}, u32[]{:S(2)}, u32[]{:S(2)}) collective-permute-start(bf16[2,96,3,128]{3,2,1,0:T(4,128)(2,1)S(1)} %get-tuple-element.97), channel_id=1, source_target_pairs={{4,0},{8,4},{12,8},{16,12},{20,16},{24,20},{28,24},{32,28},{36,32}... | collective-permute-start | bytes 442376 | tf_op jit(solution)/shard_map/ppermute | solution.py:21
  46.4 1.6 fusion.112
  48.1 0.0 copy-done.6
  48.1 2.3 %fusion.113 = f32[512,128]{1,0:T(8,128)} fusion(bf16[5376,512]{1,0:T(8,128)(2,1)S(1)} %get-tuple-element.150, bf16[5376,128]{1,0:T(8,128)(2,1)S(1)} %fusion.109), kind=kOutput, calls=%fused_computation.312 | convolution fusion | flops 704643072 | bytes 7143424 | tf_op jit(solution)/shard_map/dot_general | solution.py:42
  50.4 0.0 all-reduce.4.cloned.1.call-update
  50.4 0.7 convert_reduce_fusion.1
  51.2 0.7 slice_bitcast_fusion.50
  51.8 0.7 slice_bitcast_fusion.49
  52.5 0.6 slice_bitcast_fusion.48
  53.1 5.3 %fusion.111 = f32[128]{0:T(128)} fusion(bf16[5376,512]{1,0:T(8,128)(2,1)} %copy-done.6, bf16[512,128]{1,0:T(8,128)(2,1)} %param.19, f32[128]{0:T(128)S(1)} %copy-done.13, bf16[5376,128]{1,0:T(8,128)(2,1)} %bitcast.198), kind=kOutput, calls=%fused_computation.229 | convolution fusion | flops 707395456 | bytes 7013376 | tf_op jit(solution)/shard_map/dot_general | solution.py:62
  58.4 0.6 multiply_cosine_fusion.1
  59.1 0.0 collective-permute-done
  59.1 0.0 collective-permute-done.1
  59.1 0.1 pad_maximum_fusion.5
  59.2 1.3 collective-permute-start.2
  60.5 0.0 collective-permute-start.3
  60.5 1.6 collective-permute-done.2
  62.1 2.7 %collective-permute-done.3 = bf16[2,3,62,128]{3,2,1,0:T(8,128)(2,1)S(1)} collective-permute-done((bf16[2,3,62,128]{3,2,1,0:T(8,128)(2,1)S(1)}, bf16[2,3,62,128]{3,2,1,0:T(8,128)(2,1)S(1)}, u32[]{:S(2)}, u32[]{:S(2)}) %collective-permute-start.3) | collective-permute-done | bytes 95264 | tf_op jit(solution)/shard_map/ppermute | solution.py:21
  64.8 3.7 %maximum_select_fusion = bf16[2,102,62,128]{3,2,1,0:T(8,128)(2,1)S(1)} fusion(bf16[2,3,62,128]{3,2,1,0:T(8,128)(2,1)S(1)} %collective-permute-done.3, bf16[2,96,3,128]{3,2,1,0:T(4,128)(2,1)S(1)} %collective-permute-done.1, bf16[1,96,56,128]{3,2,1,0:T(8,128)(2,1)S(1)} %bitcast.193, bf16[1,96,56,128]{3,2,1,0:T(8,128)(2,1)S(1)} %bitcast.197, ...), kind=kLoop, calls=%fused_computation.13 | loop fusion | flops 21046272 | bytes 6475878 | tf_op jit(solution)/shard_map/jit(_where)/select_n | solution.py:94
  68.5 0.3 convert_multiply_fusion
  68.8 6.8 %fusion.8 = (f32[128]{0:T(128)S(1)}, f32[128]{0:T(128)S(1)}, f32[128]{0:T(128)S(1)}, f32[128]{0:T(128)S(1)}, f32[128]{0:T(128)S(1)}, /*index=5*/f32[128]{0:T(128...) fusion(f32[102,62,128]{2,1,0:T(8,128)S(1)} %convert_multiply_fu, ...), kind=kLoop, calls=%fused_computation.16 | loop fusion | flops 25458432 | bytes 53683200 | tf_op jit(solution)/shard_map/reduce_sum | solution.py:128
  75.6 6.7 %fusion.26 = (f32[128]{0:T(128)}, f32[128]{0:T(128)}, f32[128]{0:T(128)}, f32[128]{0:T(128)}, f32[128]{0:T(128)}, /*index=5*/f32[128]{0:T(128)}, f32[128]{0:T(12...) fusion(f32[96,56,128]{2,1,0:T(8,128)S(1)} %get-tuple-element.93, ...), kind=kLoop, calls=%fused_computation.52 | loop fusion | flops 24770304 | bytes 52306944 | tf_op jit(solution)/shard_map/reduce_sum | solution.py:128
  82.2 5.0 %fusion.44 = (f32[128]{0:T(128)}, f32[128]{0:T(128)}, f32[128]{0:T(128)}, f32[128]{0:T(128)}, f32[128]{0:T(128)}, /*index=5*/f32[128]{0:T(128)}, f32[128]{0:T(12...) fusion(f32[96,56,128]{2,1,0:T(8,128)S(1)} %get-tuple-element.93, ...), kind=kLoop, calls=%fused_computation.88 | loop fusion | flops 17889664 | bytes 38541824 | tf_op jit(solution)/shard_map/reduce_sum | solution.py:128
  87.2 0.4 fusion.110
  87.6 3.7 %stack.207 = f32[49,128]{1,0:T(8,128)S(1)} concatenate(f32[1,128]{1,0:T(1,128)} %bitcast.247, f32[1,128]{1,0:T(1,128)} %bitcast.246, f32[1,128]{1,0:T(1,128)} %bitcast.245, f32[1,128]{1,0:T(1,128)} %bitcast.244, f32[1,128]{1,0:T(1,128)} %bitcast.243, f32[1,128]{1,0:T(1,128)} %bitcast.242, f32[1,128]{1,0:T(1,128)} %bitcast.241, f32[1,128]{1,0:T(1,128)} %bitcast.240, ...), dimensions={0} | concatenate | bytes 50176 | tf_op jit(solution)/shard_map/stack | solution.py:146
  91.3 65.0 %all-reduce = (f32[49,128]{1,0:T(8,128)S(1)}, f32[128]{0:T(128)}, f32[128]{0:T(128)}, f32[128]{0:T(128)S(1)}, f32[512]{0:T(512)S(1)}, /*index=5*/f32[128]{0:T(128)S(1)}, f32[128]{0:T(128)S(1)}) all-reduce(f32[49,128]{1,0:T(8,128)S(1)} %stack.207, f32[128]{0:T(128)S(1)} %get-tuple-element.91, ...), channel_id=1, replica_groups=mesh['lon'=32,'lat'=4] {'lon','lat'}, use_global_device_ids=true, to_apply=%region_53.54 | all-reduce | flops 7424 | bytes 59392 | tf_op jit(solution)/shard_map/psum | solution.py:148
  156.3 1.2 multiply_reduce_fusion.6
  157.5 1.8 multiply_reduce_fusion.12
  159.3 1.8 multiply_reduce_fusion.11
  161.1 1.1 multiply_reduce_fusion.10
  162.3 1.1 multiply_reduce_fusion.9
  163.4 19.6 %fusion.60 = bf16[96,56,128]{2,1,0:T(8,128)(2,1)} fusion(f32[102,62,128]{2,1,0:T(8,128)S(1)} %fusion.110, bf16[96,56,128]{2,1,0:T(8,128)(2,1)} %param.13, f32[128]{0:T(128)} %get-tuple-element.145, f32[128]{0:T(128)} %get-tuple-element.146, f32[128]{0:T(128)} %get-tuple-element.99, f32[128]{0:T(128)} %get-tuple-element.100, f32[128]{0:T(128)} %get-tuple-element.101, ...), kind=kLoop, calls=%fused_computation.117 | loop fusion | flops 69500928 | bytes 137651072 | tf_op jit(solution)/shard_map/convert_element_type | solution.py:143
  182.9 1.2 multiply_reduce_fusion.8
  186.7 1.2 multiply_reduce_fusion.7
  187.9 5.6 %all-reduce.4.cloned.1.call-done = (f32[128,512]{1,0:T(8,128)}, f32[512,128]{1,0:T(8,128)}) async-done(((f32[128,512]{1,0:T(8,128)}, f32[512,128]{1,0:T(8,128)}), (f32[128,512]{1,0:T(8,128)}, f32[512,128]{1,0:T(8,128)})) %all-reduce.4.cloned.1.call-update) | async-done | bytes 524304 | tf_op jit(solution)/shard_map/psum | solution.py:148
  193.4 2.3 %multiply_reduce_fusion.5 = (f32[]{:T(128)}, f32[128,512]{1,0:T(8,128)}) fusion(f32[128,512]{1,0:T(8,128)} %get-tuple-element.71), kind=kLoop, calls=%fused_computation.232 | loop fusion | flops 196607 | bytes 524292 | tf_op jit(solution)/shard_map/reduce_sum | solution.py:150
  195.7 2.3 %multiply_reduce_fusion.4 = (f32[]{:T(128)}, f32[512,128]{1,0:T(8,128)}) fusion(f32[512,128]{1,0:T(8,128)} %get-tuple-element.72), kind=kLoop, calls=%fused_computation.231 | loop fusion | flops 196607 | bytes 524292 | tf_op jit(solution)/shard_map/reduce_sum | solution.py:150
  (18 shorter events, 0.1 us)
Async XLA Ops:
  7.2 8.7 %copy-start = (bf16[128,512]{1,0:T(8,128)(2,1)S(1)}, bf16[128,512]{1,0:T(8,128)(2,1)}, u32[]{:S(2)}) copy-start(bf16[128,512]{1,0:T(8,128)(2,1)} %param.17) | copy-start | bytes 393220
  7.2 5.6 %copy-start.1 = (bf16[96,56,128]{2,1,0:T(8,128)(2,1)S(1)}, bf16[96,56,128]{2,1,0:T(8,128)(2,1)}, u32[]{:S(2)}) copy-start(bf16[96,56,128]{2,1,0:T(8,128)(2,1)} %param.12) | copy-start | bytes 4128772
  7.2 5.3 %copy-start.4 = (bf16[96,56,128]{2,1,0:T(8,128)(2,1)S(1)}, bf16[96,56,128]{2,1,0:T(8,128)(2,1)}, u32[]{:S(2)}) copy-start(bf16[96,56,128]{2,1,0:T(8,128)(2,1)} %param.13) | copy-start | bytes 4128772
  7.2 5.3 %copy-start.9 = (f32[128]{0:T(128)S(1)}, f32[128]{0:T(128)}, u32[]{:S(2)}) copy-start(f32[128]{0:T(128)} %param.21) | copy-start | bytes 1540
  7.2 5.6 %copy-start.8 = (f32[128]{0:T(128)S(1)}, f32[128]{0:T(128)}, u32[]{:S(2)}) copy-start(f32[128]{0:T(128)} %param.15) | copy-start | bytes 1540
  7.2 5.6 %copy-start.10 = (f32[128]{0:T(128)S(1)}, f32[128]{0:T(128)}, u32[]{:S(2)}) copy-start(f32[128]{0:T(128)} %param.16) | copy-start | bytes 1540
  7.2 186.2 %all-reduce.4.cloned.1.call-start = ((), (), s32[]{:S(2)}) async-start(), calls=%async_computation | async-start | bytes 1048576 | tf_op jit(solution)/shard_map/psum | solution.py:148
  12.5 3.3 %copy-start.12 = (f32[512]{0:T(512)S(1)}, f32[512]{0:T(512)}, u32[]{:S(2)}) copy-start(f32[512]{0:T(512)} %param.18) | copy-start | bytes 6148
  15.9 4.2 %copy-start.11 = (bf16[512,128]{1,0:T(8,128)(2,1)S(1)}, bf16[512,128]{1,0:T(8,128)(2,1)}, u32[]{:S(2)}) copy-start(bf16[512,128]{1,0:T(8,128)(2,1)} %param.19) | copy-start | bytes 393220
  20.1 28.0 %copy-start.6 = (bf16[5376,512]{1,0:T(8,128)(2,1)}, bf16[5376,512]{1,0:T(8,128)(2,1)S(1)}, u32[]{:S(2)}) copy-start(bf16[5376,512]{1,0:T(8,128)(2,1)S(1)} %get-tuple-element.150) | copy-start | bytes 16515076
  32.2 4.0 %copy-start.2 = (bf16[96,56,128]{2,1,0:T(8,128)(2,1)S(1)}, bf16[96,56,128]{2,1,0:T(8,128)(2,1)}, u32[]{:S(2)}) copy-start(bf16[96,56,128]{2,1,0:T(8,128)(2,1)} %param.11) | copy-start | bytes 4128772
  37.0 22.1 %collective-permute-start = (bf16[2,96,3,128]{3,2,1,0:T(4,128)(2,1)}, bf16[2,96,3,128]{3,2,1,0:T(4,128)(2,1)S(1)}, u32[]{:S(2)}, u32[]{:S(2)}) collective-permute-start(bf16[2,96,3,128]{3,2,1,0:T(4,128)(2,1)} %get-tuple-element.96), channel_id=1, source_target_pairs={{0,4},{4,8},{8,12},{12,16},{16,20},{20,24},{24,28},{28,32},{32,36}... | collective-permute-start | bytes 442376 | tf_op jit(solution)/shard_map/ppermute | solution.py:20
  40.8 18.3 %collective-permute-start.1 = (bf16[2,96,3,128]{3,2,1,0:T(4,128)(2,1)S(1)}, bf16[2,96,3,128]{3,2,1,0:T(4,128)(2,1)S(1)}, u32[]{:S(2)}, u32[]{:S(2)}) collective-permute-start(bf16[2,96,3,128]{3,2,1,0:T(4,128)(2,1)S(1)} %get-tuple-element.97), channel_id=1, source_target_pairs={{4,0},{8,4},{12,8},{16,12},{20,16},{24,20},{28,24},{32,28},{36,32}... | collective-permute-start | bytes 442376 | tf_op jit(solution)/shard_map/ppermute | solution.py:21
  48.1 2.4 %copy-start.5 = (bf16[96,56,128]{2,1,0:T(8,128)(2,1)S(1)}, bf16[96,56,128]{2,1,0:T(8,128)(2,1)}, u32[]{:S(2)}) copy-start(bf16[96,56,128]{2,1,0:T(8,128)(2,1)} %param.13) | copy-start | bytes 4128772
  48.1 3.1 %copy-start.7 = (f32[49,128]{1,0:T(8,128)S(1)}, f32[49,128]{1,0:T(8,128)}, u32[]{:S(2)}) copy-start(f32[49,128]{1,0:T(8,128)} %param.14) | copy-start | bytes 75268
  48.1 5.1 %copy-start.13 = (f32[128]{0:T(128)S(1)}, f32[128]{0:T(128)}, u32[]{:S(2)}) copy-start(f32[128]{0:T(128)} %param.20) | copy-start | bytes 1540
  53.1 6.0 %copy-start.3 = (bf16[96,56,128]{2,1,0:T(8,128)(2,1)S(1)}, bf16[96,56,128]{2,1,0:T(8,128)(2,1)}, u32[]{:S(2)}) copy-start(bf16[96,56,128]{2,1,0:T(8,128)(2,1)} %param.11) | copy-start | bytes 4128772
  59.2 2.9 %collective-permute-start.2 = (bf16[2,3,62,128]{3,2,1,0:T(8,128)(2,1)S(1)}, bf16[2,3,62,128]{3,2,1,0:T(8,128)(2,1)S(1)}, u32[]{:S(2)}, u32[]{:S(2)}) collective-permute-start(bf16[2,3,62,128]{3,2,1,0:T(8,128)(2,1)S(1)} %get-tuple-element.94), channel_id=1, source_target_pairs={{0,1},{1,2},{2,3},{3,0},{4,5},{5,6},{6,7},{7,4},{8,9},{9,10},{10,1... | collective-permute-start | bytes 285704 | tf_op jit(solution)/shard_map/ppermute | solution.py:20
  60.5 4.3 %collective-permute-start.3 = (bf16[2,3,62,128]{3,2,1,0:T(8,128)(2,1)S(1)}, bf16[2,3,62,128]{3,2,1,0:T(8,128)(2,1)S(1)}, u32[]{:S(2)}, u32[]{:S(2)}) collective-permute-start(bf16[2,3,62,128]{3,2,1,0:T(8,128)(2,1)S(1)} %get-tuple-element.95), channel_id=1, source_target_pairs={{1,0},{2,1},{3,2},{0,3},{5,4},{6,5},{7,6},{4,7},{9,8},{10,9},{11,1... | collective-permute-start | bytes 285704 | tf_op jit(solution)/shard_map/ppermute | solution.py:21
Sparse Core Ops, SparseCore 0:
  50.5 142.8 all-reduce.3
where the time goes:
time: 210 us; the launch traced here: 209 us
  other arithmetic  71 us (34%)
  blocking collectives  65 us (31%)
  matrix products  25.5 us (12%)
  between operations  21.3 us (10%)
  starting transfers between devices  10.8 us (5%)
  waiting for transfers between devices  9.86 us (5%)
  local copies, waits for them, and re-layouts  5.89 us (3%)
    psum x1, blocking collectives, on_device(): totals = lax.psum(locals_all, ('lon', 'lat'))  65 us
    convert_element_type x1, other arithmetic, on_device(): (cotangent.astype(jnp.float32) + row_cos[:, None, None] * conv_sum).astyp...  19.6 us
    reduce_sum x3, other arithmetic, on_device(): jnp.sum(inner * weighted[3 + lat_off:3 + lat_off + rows, 3 + lon_off:3 +...  18.4 us
    reduce_sum x9, other arithmetic, on_device(): grad_norm = jnp.sqrt(sum((jnp.sum(part * part) for part in scaled)))  14 us
    dot_general x2, matrix products, contract_last(): lax.dot_general(left, right, (((1,), (1,)), ((), ())), preferred_element_...  12.1 us
    ppermute x2, starting transfers between devices, extended(): after = lax.ppermute(leading, axis, down)  5.67 us
    psum x1, waiting for transfers between devices, on_device(): totals = lax.psum(locals_all, ('lon', 'lat'))  5.56 us
    dot_general x1, matrix products, channel_backward(): out = jnp.dot(act, w_out, preferred_element_type=jnp.float32) + b_out  5.25 us
  transfers between devices with their start and end apart: 5, of which 3 were waited for; matrix products, arithmetic and copies ran while one was open for 33% of the time, Pallas kernels for 0%

commit v1 on v0

v1 whole, which is shorter than its diff:
```python
import math

import jax
import jax.numpy as jnp
import ml_dtypes
import numpy as np
from jax import lax
from jax.experimental import pallas as pl
from jax.experimental.pallas import tpu as pltpu
from jax.sharding import PartitionSpec as P

MESH = pl.DeviceIdType.MESH
f32, bf16 = jnp.float32, jnp.bfloat16
EPS = 1e-06
COEF = 0.044715
ROOT = math.sqrt(2.0 / math.pi)

N = 14
OUT = 8
PAIRS = 104
FREQ = 2 * PAIRS
SCALE = 1.828125
LAT_ROWS, COLS, CH, HID, TAPS = 96, 56, 128, 512, 49
TL, TC = LAT_ROWS // OUT, COLS // OUT
CHUNK = 32
SUB = 896
SMALL = 64


def tables():
    own = [(0, 0), (0, 7), (7, 0), (7, 7)]
    seen, pairs = set(own), []
    for k in range(N):
        for l in range(N):
            if (k, l) not in seen:
                seen.add((k, l))
                seen.add(((-k) % N, (-l) % N))
                pairs.append((k, l))
    freq = np.array(own + pairs)
    weight = np.array([1.0] * 4 + [2.0] * 96)[:, None] / (N * N)
    twin = np.array([0.0] * 4 + [1.0] * 96)[:, None]

    def angle(rows, cols, row_off, col_off):
        m, n = np.meshgrid(np.arange(rows) + row_off, np.arange(cols) + col_off, indexing="ij")
        m, n = m.ravel(), n.ravel()
        return 2 * np.pi * ((np.outer(freq[:, 0], m) + np.outer(freq[:, 1], n)) % N) / N

    def interleave(re, im):
        fill = np.zeros((PAIRS - 100, re.shape[1]))
        re, im = np.concatenate([re, fill]), np.concatenate([im, fill])
        shape = (PAIRS // 8, 8, re.shape[1])
        return np.stack([re.reshape(shape), im.reshape(shape)], 1).reshape(FREQ, -1)

    inside = np.tile(np.array([0.0] + [1.0] * 14 + [0.0]), N)
    a = angle(N, 16, 0, -1)
    fwd = interleave(np.cos(a) * inside, -np.sin(a) * inside * twin)
    a = angle(OUT, OUT, 6, 6)
    fwd_tile = interleave(np.cos(a), -np.sin(a) * twin)
    inv = interleave(np.cos(a) * weight, -np.sin(a) * weight * twin).T
    a = angle(7, 7, 0, 0)
    taps = interleave(np.cos(a), -np.sin(a) * twin)
    taps_inv = interleave(np.cos(a) * weight, -np.sin(a) * weight * twin).T
    area = N * N
    return (
        (fwd * SCALE).astype(ml_dtypes.bfloat16),
        (fwd_tile * SCALE).astype(ml_dtypes.bfloat16),
        (inv * area * SCALE).astype(ml_dtypes.bfloat16),
        (np.pad(taps, ((0, 0), (0, 7))) / (area * SCALE * SCALE)).astype(np.float32),
        (np.pad(taps_inv, ((0, 7), (0, 0))) / (SCALE * SCALE)).astype(np.float32),
    )


def dot(a, b):
    return jnp.dot(a, b, preferred_element_type=f32)


def dot_exact(a, b):
    return jnp.dot(a, b, preferred_element_type=f32, precision=lax.Precision.HIGHEST)


def dot_last(a, b):
    return lax.dot_general(a, b, (((1,), (1,)), ((), ())), preferred_element_type=f32)


def dot_rows(a, b):
    return lax.dot_general(a, b, (((0,), (0,)), ((), ())), preferred_element_type=f32)


def rows8(v):
    return jnp.sum(v.reshape(v.shape[0] // 8, 8, v.shape[1]), 0)


def make_kernel(nz, nx, nyh, nyl, ncore, total_cells):
    nlon, nlat = nz * nx * nyh, nyl * ncore
    ny = nyh * nyl
    nb, na = nz * ny, nx * ncore
    wrows = 2 * CH // nb
    cells = LAT_ROWS * COLS
    step = CHUNK * COLS
    steps = LAT_ROWS // CHUNK
    factor = float(total_cells) ** (-0.5)

    def kernel(
        x_hbm, c_hbm, f_hbm, ker_ref, gain_ref, bias_ref, win_ref, bin_ref, wout_ref, bout_ref, ls_ref,
        cos_ref, mf_ref, mg_ref, mi_ref, mk_ref, md_ref,
        out_hbm, dk_ref, dcb_ref, dgain_ref, dbias_ref, dwin_ref, dbin_ref, dwout_ref, dbout_ref, dls_ref, norm_ref,
        xv, cv, fv, outv, dup, fs, yb, kpad, kh, acc, gw, gbin, small, sm32,
        hs, hr, vs, vr, ws, wr, w2, wf, s1, s2,
        in_sem, out_sem, h_send, h_recv, v_send, v_recv,
        w1_send, w1_recv, w2_send, w2_recv, w3_send, w3_recv, s1_send, s1_recv, s2_send, s2_recv,
    ):
        lon, lat = lax.axis_index("lon"), lax.axis_index("lat")
        z, x, yh = lax.div(lon, nx * nyh), lax.rem(lax.div(lon, nyh), nx), lax.rem(lon, nyh)
        yl, core = lax.div(lat, ncore), lax.rem(lat, ncore)
        b_me = z * ny + yh * nyl + yl
        a_me = x * ncore + core

        def b_peer(b):
            bz, by = lax.div(b, ny), lax.rem(b, ny)
            return (bz * (nx * nyh) + x * nyh + lax.div(by, nyl), lax.rem(by, nyl) * ncore + core)

        def a_peer(a):
            return (z * (nx * nyh) + lax.div(a, ncore) * nyh + yh, yl * ncore + lax.rem(a, ncore))

        right, left = lax.rem(lon + 1, nlon), lax.rem(lon + nlon - 1, nlon)
        down, up = lax.rem(lat + 1, nlat), lax.rem(lat + nlat - 1, nlat)

        def load(i, which):
            src, dst = ((x_hbm, xv), (c_hbm, cv), (f_hbm, fv))[which]
            rows = pl.ds(i * step, step)
            return pltpu.make_async_copy(src.at[rows], dst.at[rows], in_sem.at[which, i])

        for i in range(steps):
            for which in range(3):
                load(i, which).start()

        barrier = pltpu.get_barrier_semaphore()
        for peer in ((right, lat), (left, lat), (lon, down), (lon, up)):
            pl.semaphore_signal(barrier, inc=1, device_id=peer, device_id_type=MESH)

        def greet_b(d, carry):
            pl.semaphore_signal(barrier, inc=1, device_id=b_peer(lax.rem(b_me + d, nb)), device_id_type=MESH)
            return carry

        def greet_a(d, carry):
            pl.semaphore_signal(barrier, inc=1, device_id=a_peer(lax.rem(a_me + d, na)), device_id_type=MESH)
            return carry

        lax.fori_loop(1, nb, greet_b, 0)
        lax.fori_loop(1, na, greet_a, 0)

        third = jnp.full((CH, CH), 1.0 / CH, bf16)
        none = jnp.zeros((CH, CH), bf16)
        mean_two = jnp.concatenate(
            [jnp.concatenate([third, none], 1), jnp.concatenate([none, third], 1)], 0
        )
        gain, bias, scale = gain_ref[...], bias_ref[...], ls_ref[...]
        gw[...] = jnp.zeros_like(gw)
        gbin[...] = jnp.zeros_like(gbin)
        small[...] = jnp.zeros_like(small)
        acc[...] = jnp.zeros_like(acc)
        kpad[...] = jnp.zeros_like(kpad)
        kpad[0:TAPS] = ker_ref[...]
        kh[...] = dot_exact(mk_ref[...], kpad[...])

        def mlp(i, carry):
            for which in range(3):
                rows_hbm = pl.ds(pl.multiple_of(i * step, step), step)
                src, dst = ((x_hbm, xv), (c_hbm, cv), (f_hbm, fv))[which]
                pltpu.make_async_copy(src.at[rows_hbm], dst.at[rows_hbm], in_sem.at[which, i]).wait()
            rows = pl.ds(pl.multiple_of(i * step, step), step)
            xb, cb = xv[rows, :], cv[rows, :]
            center = xb.astype(f32) - dot(xb, third)
            rstd = lax.rsqrt(dot((center * center).astype(bf16), third) + EPS)
            normed = center * rstd
            zed = (normed * gain + bias).astype(bf16)
            cot = cb.astype(f32)
            d_out = (cot * scale).astype(bf16)
            acts, dpres = [], []
            g_bin = jnp.zeros((8, HID), f32)
            for s in range(0, step, SUB):
                h = dot(zed[s : s + SUB], win_ref[...]) + bin_ref[...]
                d_act = dot_last(d_out[s : s + SUB], wout_ref[...])
                h2 = h * h
                inner = h * (ROOT + (ROOT * COEF) * h2)
                wide = h * (2 * ROOT + (6 * ROOT * COEF) * h2)
                gate = 0.5 * jnp.tanh(inner) + 0.5
                d_pre = d_act * (gate * (1.0 + (1.0 - gate) * wide))
                g_bin = g_bin + rows8(d_pre)
                acts.append((h * gate).astype(bf16))
                dpres.append(d_pre.astype(bf16))
            act, d_pre = jnp.concatenate(acts, 0), jnp.concatenate(dpres, 0)
            gbin[...] += g_bin
            gw[CH:, :] += dot_rows(cb, act)
            gw[:CH, :] += dot_rows(zed, d_pre)
            d_zed = dot_last(d_pre, win_ref[...])
            d_gain = d_zed * normed
            d_norm = d_zed * gain
            means = dot(
                jnp.concatenate([d_norm.astype(bf16), (d_gain * gain).astype(bf16)], 1), mean_two
            )
            du = rstd * (d_norm - means[:, :CH] - normed * means[:, CH:])
            dup[pl.ds(3 + i * CHUNK, CHUNK), 4 : 4 + COLS, :] = du.reshape(CHUNK, COLS, CH)
            small[0] += rows8(d_gain)
            small[1] += rows8(d_zed)
            small[2] += rows8(du)
            small[3] += rows8(cot)
            field = fv[rows, :].astype(f32).reshape(CHUNK, COLS, CH)
            for r in range(CHUNK):
                fs[i * CHUNK + r] = field[r] * cos_ref[lat * LAT_ROWS + i * CHUNK + r]
            return carry

        lax.fori_loop(0, steps, mlp, 0)

        half = LAT_ROWS // 2
        low = lax.broadcasted_iota(jnp.int32, (half, 8, CH), 1) < 4

        def copy_h(side):
            return pltpu.make_async_remote_copy(
                src_ref=hs.at[side], dst_ref=hr.at[side], send_sem=h_send.at[side], recv_sem=h_recv.at[side],
                device_id=((right, lat), (left, lat))[side], device_id_type=MESH,
            )

        def copy_v(side):
            return pltpu.make_async_remote_copy(
                src_ref=vs.at[side], dst_ref=vr.at[side], send_sem=v_send.at[side], recv_sem=v_recv.at[side],
                device_id=((lon, down), (lon, up))[side], device_id_type=MESH,
            )

        pl.semaphore_wait(barrier, 4 + (nb - 1) + (na - 1))
        first, second = dup[3 : 3 + half, 56:64, :], dup[3 + half : 3 + LAT_ROWS, 56:64, :]
        hs[0] = jnp.where(low, first, pltpu.roll(second, 4, 1)).reshape(half * 8, CH).astype(bf16)
        copy_h(0).start()
        first, second = dup[3 : 3 + half, 0:8, :], dup[3 + half : 3 + LAT_ROWS, 0:8, :]
        hs[1] = jnp.where(low, pltpu.roll(second, 4, 1), first).reshape(half * 8, CH).astype(bf16)
        copy_h(1).start()

        def copy_w1(b_to, b_from):
            return pltpu.make_async_remote_copy(
                src_ref=ws.at[b_to], dst_ref=wr.at[b_from], send_sem=w1_send.at[b_to], recv_sem=w1_recv.at[b_from],
                device_id=b_peer(b_to), device_id_type=MESH,
            )

        ws[...] = gw[...].astype(bf16).reshape(nb, wrows, HID)

        def send_w1(d, carry):
            copy_w1(lax.rem(b_me + d, nb), b_me).start()
            return carry

        lax.fori_loop(1, nb, send_w1, 0)

        def tile_pair(slot, i0, i1, t):
            def window(i):
                return dup[pl.ds(i * OUT, N), 8 * t : 8 * t + 16, :].reshape(N * 16, CH).astype(bf16)

            def field(i):
                return fs[pl.ds(i * OUT, OUT), 8 * t : 8 * t + 8, :].reshape(OUT * OUT, CH).astype(bf16)

            shape = (PAIRS // 8, 2, 8, 2 * CH)
            w = dot(mf_ref[...], jnp.concatenate([window(i0), window(i1)], 1)).reshape(shape)
            g = dot(mg_ref[...], jnp.concatenate([field(i0), field(i1)], 1)).reshape(shape)
            k = kh[...].reshape(PAIRS // 8, 2, 8, CH)
            k = jnp.concatenate([k, k], -1)
            w_re, w_im, g_re, g_im, k_re, k_im = w[:, 0], w[:, 1], g[:, 0], g[:, 1], k[:, 0], k[:, 1]
            y = jnp.stack([k_re * w_re - k_im * w_im, k_re * w_im + k_im * w_re], 1)
            yb[slot] = y.reshape(FREQ, 2 * CH).astype(bf16)
            d = jnp.stack([g_re * w_re + g_im * w_im, g_im * w_re - g_re * w_im], 1).reshape(FREQ, 2 * CH)
            acc[...] += d[:, :CH] + d[:, CH:]

        def middle(j, carry):
            for t in range(1, TC - 1):
                tile_pair(j * TC + t, 1 + 2 * j, 2 + 2 * j, t)
            return carry

        def sides(j, carry):
            for t in (0, TC - 1):
                tile_pair(j * TC + t, 1 + 2 * j, 2 + 2 * j, t)
            return carry

        lax.fori_loop(0, 3, middle, 0)

        copy_h(0).wait_recv()
        copy_h(1).wait_recv()
        near = hr[0].astype(f32).reshape(half, 8, CH)
        dup[3 : 3 + half, 0:8, :] = jnp.where(low, near, dup[3 : 3 + half, 0:8, :])
        dup[3 + half : 3 + LAT_ROWS, 0:8, :] = jnp.where(
            low, pltpu.roll(near, 4, 1), dup[3 + half : 3 + LAT_ROWS, 0:8, :]
        )
        near = hr[1].astype(f32).reshape(half, 8, CH)
        dup[3 : 3 + half, 56:64, :] = jnp.where(low, dup[3 : 3 + half, 56:64, :], near)
        dup[3 + half : 3 + LAT_ROWS, 56:64, :] = jnp.where(
            low, dup[3 + half : 3 + LAT_ROWS, 56:64, :], pltpu.roll(near, 4, 1)
        )
        vs[0] = dup[LAT_ROWS : LAT_ROWS + 3].reshape(192, CH).astype(bf16)
        vs[1] = dup[3:6].reshape(192, CH).astype(bf16)
        copy_v(0).start()
        copy_v(1).start()

        lax.fori_loop(3, 5, middle, 0)

        def copy_w2(a_to, a_from):
            return pltpu.make_async_remote_copy(
                src_ref=w2.at[a_me], dst_ref=w2.at[a_from], send_sem=w2_send.at[a_to], recv_sem=w2_recv.at[a_from],
                device_id=a_peer(a_to), device_id_type=MESH,
            )

        wr[b_me] = ws[b_me]

        def wait_w1(d, carry):
            b = lax.rem(b_me + d, nb)
            copy_w1(b, b).wait_recv()
            return carry

        lax.fori_loop(1, nb, wait_w1, 0)
        w2[a_me] = jnp.sum(wr[...].astype(f32), 0).astype(bf16)

        def send_w2(d, carry):
            copy_w2(lax.rem(a_me + d, na), a_me).start()
            return carry

        lax.fori_loop(1, na, send_w2, 0)

        lax.fori_loop(0, 5, sides, 0)

        copy_v(0).wait_recv()
        copy_v(1).wait_recv()
        zero = jnp.zeros((3, 64, CH), f32)
        dup[0:3] = jnp.where(lat > 0, vr[0].astype(f32).reshape(3, 64, CH), zero)
        dup[LAT_ROWS + 3 : LAT_ROWS + 6] = jnp.where(lat < nlat - 1, vr[1].astype(f32).reshape(3, 64, CH), zero)
        for t in range(TC):
            tile_pair(5 * TC + t, 0, TL - 1, t)

        sm32[...] = jnp.zeros_like(sm32)
        sm32[0:56] = dot_exact(md_ref[...], acc[...])
        total = jnp.sum(gbin[...], 0, keepdims=True)
        for q in range(4):
            sm32[49 + q : 50 + q] = total[:, q * CH : (q + 1) * CH]
            sm32[53 + q : 54 + q] = jnp.sum(small[q], 0, keepdims=True)
        s1[a_me] = sm32[...].astype(bf16)

        def copy_s1(a_to, a_from):
            return pltpu.make_async_remote_copy(
                src_ref=s1.at[a_me], dst_ref=s1.at[a_from], send_sem=s1_send.at[a_to], recv_sem=s1_recv.at[a_from],
                device_id=a_peer(a_to), device_id_type=MESH,
            )

        def copy_s2(b_to, b_from):
            return pltpu.make_async_remote_copy(
                src_ref=s2.at[b_me], dst_ref=s2.at[b_from], send_sem=s2_send.at[b_to], recv_sem=s2_recv.at[b_from],
                device_id=b_peer(b_to), device_id_type=MESH,
            )

        def copy_w3(b_to, b_from):
            return pltpu.make_async_remote_copy(
                src_ref=wf.at[b_me], dst_ref=wf.at[b_from], send_sem=w3_send.at[b_to], recv_sem=w3_recv.at[b_from],
                device_id=b_peer(b_to), device_id_type=MESH,
            )

        def over_a(copy, act):
            def body(d, carry):
                peer = lax.rem(a_me + d, na)
                if act == "send":
                    copy(peer, a_me).start()
                elif act == "recv":
                    copy(peer, peer).wait_recv()
                else:
                    copy(peer, a_me).wait_send()
                return carry

            lax.fori_loop(1, na, body, 0)

        def over_b(copy, act):
            def body(d, carry):
                peer = lax.rem(b_me + d, nb)
                if act == "send":
                    copy(peer, b_me).start()
                elif act == "recv":
                    copy(peer, peer).wait_recv()
                else:
                    copy(peer, b_me).wait_send()
                return carry

            lax.fori_loop(1, nb, body, 0)

        over_a(copy_s1, "send")
        over_a(copy_w2, "recv")
        wf[b_me] = jnp.sum(w2[...].astype(f32), 0).astype(bf16)

        def store(i):
            rows = pl.ds(i * (OUT * COLS), OUT * COLS)
            return pltpu.make_async_copy(outv.at[rows], out_hbm.at[rows], out_sem.at[i])

        def finish_pair(j, i0, i1):
            tiles = [dot(mi_ref[...], yb[j * TC + t]).reshape(OUT, OUT, 2 * CH) for t in range(TC)]
            conv = jnp.concatenate(tiles, 1)
            for n, i in ((0, i0), (1, i1)):
                rows = pl.ds(pl.multiple_of(i * (OUT * COLS), OUT * COLS), OUT * COLS)
                cot = cv[rows, :].astype(f32).reshape(OUT, COLS, CH)
                part = conv[:, :, n * CH : (n + 1) * CH]
                value = [cot[r] + part[r] * cos_ref[lat * LAT_ROWS + i * OUT + r] for r in range(OUT)]
                outv[rows, :] = jnp.concatenate(value, 0).astype(bf16)
                store(i).start()

        def finish(j, carry):
            finish_pair(j, 1 + 2 * j, 2 + 2 * j)
            return carry

        over_a(copy_s1, "recv")
        s2[b_me] = jnp.sum(s1[...].astype(f32), 0).astype(bf16)
        over_b(copy_s2, "send")
        over_b(copy_w3, "send")
        lax.fori_loop(0, 5, finish, 0)
        finish_pair(5, 0, TL - 1)

        over_b(copy_w3, "recv")
        d_win = jnp.concatenate([wf[b].astype(f32) for b in range(nb // 2)], 0) * factor
        dwin_ref[...] = d_win
        g_out = jnp.concatenate([wf[b].astype(f32) for b in range(nb // 2, nb)], 0) * factor
        g_out = g_out.T
        d_wout = g_out * scale
        dwout_ref[...] = d_wout
        over_b(copy_s2, "recv")
        sums = jnp.sum(s2[...].astype(f32), 0) * factor
        sm32[...] = sums
        dk = sm32[0:TAPS]
        d_bin = jnp.concatenate([sm32[49 + q : 50 + q] for q in range(4)], 1)
        d_gain, d_bias, d_cb, s_cot = (sm32[53 + q : 54 + q] for q in range(4))
        d_bout = s_cot * scale
        d_ls = jnp.sum(g_out * wout_ref[...].astype(f32), 0, keepdims=True) + bout_ref[...] * s_cot
        dk_ref[...] = dk
        dbin_ref[...] = d_bin
        dgain_ref[...] = d_gain
        dbias_ref[...] = d_bias
        dcb_ref[...] = d_cb
        dbout_ref[...] = d_bout
        dls_ref[...] = d_ls
        squares = jnp.sum(d_win * d_win, 0, keepdims=True) + jnp.sum(d_bin * d_bin, 0, keepdims=True)
        squares = sum(squares[:, q * CH : (q + 1) * CH] for q in range(4))
        squares = squares + jnp.sum(d_wout * d_wout, 0, keepdims=True) + jnp.sum(dk * dk, 0, keepdims=True)
        for part in (d_gain, d_bias, d_cb, d_bout, d_ls):
            squares = squares + part * part
        norm_ref[...] = jnp.sqrt(jnp.sum(squares, 1, keepdims=True))

        for side in range(2):
            copy_h(side).wait_send()
            copy_v(side).wait_send()
        over_b(copy_w1, "done")
        over_a(copy_w2, "done")
        over_b(copy_w3, "done")
        over_a(copy_s1, "done")
        over_b(copy_s2, "done")

        def drain(i, carry):
            store(i).wait()
            return carry

        lax.fori_loop(0, TL, drain, 0)

    hbm, vmem, smem = (pl.BlockSpec(memory_space=m) for m in (pl.ANY, pltpu.VMEM, pltpu.SMEM))
    shape = jax.ShapeDtypeStruct
    dma = pltpu.SemaphoreType.DMA
    return pl.pallas_call(
        kernel,
        in_specs=[hbm] * 3 + [vmem] * 8 + [smem] + [vmem] * 5,
        out_specs=[hbm] + [vmem] * 10,
        out_shape=[
            shape((cells, CH), bf16),
            shape((TAPS, CH), f32),
            shape((1, CH), f32),
            shape((1, CH), f32),
            shape((1, CH), f32),
            shape((CH, HID), f32),
            shape((1, HID), f32),
            shape((HID, CH), f32),
            shape((1, CH), f32),
            shape((1, CH), f32),
            shape((1, 1), f32),
        ],
        scratch_shapes=[
            pltpu.VMEM((cells, CH), bf16),
            pltpu.VMEM((cells, CH), bf16),
            pltpu.VMEM((cells, CH), bf16),
            pltpu.VMEM((cells, CH), bf16),
            pltpu.VMEM((LAT_ROWS + 6, COLS + 8, CH), f32),
            pltpu.VMEM((LAT_ROWS, COLS, CH), f32),
            pltpu.VMEM((TL * TC // 2, FREQ, 2 * CH), bf16),
            pltpu.VMEM((56, CH), f32),
            pltpu.VMEM((FREQ, CH), f32),
            pltpu.VMEM((FREQ, CH), f32),
            pltpu.VMEM((2 * CH, HID), f32),
            pltpu.VMEM((8, HID), f32),
            pltpu.VMEM((4, 8, CH), f32),
            pltpu.VMEM((SMALL, CH), f32),
            pltpu.VMEM((2, LAT_ROWS * 4, CH), bf16),
            pltpu.VMEM((2, LAT_ROWS * 4, CH), bf16),
            pltpu.VMEM((2, 192, CH), bf16),
            pltpu.VMEM((2, 192, CH), bf16),
            pltpu.VMEM((nb, wrows, HID), bf16),
            pltpu.VMEM((nb, wrows, HID), bf16),
            pltpu.VMEM((na, wrows, HID), bf16),
            pltpu.VMEM((nb, wrows, HID), bf16),
            pltpu.VMEM((na, SMALL, CH), bf16),
            pltpu.VMEM((nb, SMALL, CH), bf16),
            dma((3, steps)),
            dma((TL,)),
            dma((2,)),
            dma((2,)),
            dma((2,)),
            dma((2,)),
            dma((nb,)),
            dma((nb,)),
            dma((na,)),
            dma((na,)),
            dma((nb,)),
            dma((nb,)),
            dma((na,)),
            dma((na,)),
            dma((nb,)),
            dma((nb,)),
        ],
        compiler_params=pltpu.CompilerParams(
            collective_id=0, has_side_effects=True, vmem_limit_bytes=60 * 2**20
        ),
        cost_estimate=pl.CostEstimate(flops=6 * 10**9, bytes_accessed=6 * 10**6, transcendentals=3 * 10**6),
        name="block_backward",
    )


def solution(mesh):
    nlon, nlat = mesh.shape["lon"], mesh.shape["lat"]
    nz, nx, nyh = (4, 4, 2) if nlon == 32 else (nlon, 1, 1)
    nyl, ncore = nlat // 2, 2
    total_rows, total_cols = LAT_ROWS * nlat, COLS * nlon
    call = make_kernel(nz, nx, nyh, nyl, ncore, total_rows * total_cols)
    fwd, fwd_tile, inv, taps, taps_inv = tables()
    place = (np.arange(total_rows, dtype=np.float32) + np.float32(0.5)) / np.float32(total_rows) - np.float32(0.5)
    weight = np.cos(np.float32(math.pi) * place).astype(np.float32)

    def on_device(field_in, conv_out, cotangent, kernel, ln_gain, ln_bias, w_in, b_in, w_out, b_out, layer_scale):
        rows, cols, width = conv_out.shape
        flat = lambda v: v.reshape(rows * cols, width)
        line = lambda v: v.reshape(1, -1)
        outs = call(
            flat(conv_out), flat(cotangent), flat(field_in), kernel, line(ln_gain), line(ln_bias), w_in, line(b_in),
            w_out, line(b_out), line(layer_scale), weight, fwd, fwd_tile, inv, taps, taps_inv,
        )
        d_field, d_kernel, d_cb, d_gain, d_bias, d_win, d_bin, d_wout, d_bout, d_ls, norm = outs
        wide = lambda v: v.reshape(-1)
        return (
            d_field.reshape(rows, cols, width), d_kernel, wide(d_cb), wide(d_gain), wide(d_bias), d_win, wide(d_bin),
            d_wout, wide(d_bout), wide(d_ls), norm.reshape(()),
        )

    grid = P("lat", "lon", None)
    return jax.shard_map(
        on_device,
        mesh=mesh,
        in_specs=(grid, grid, grid) + (P(),) * 8,
        out_specs=(grid,) + (P(),) * 10,
        check_vma=False,
    )
```

time: 210 us -> 59.8 us (0.28)
  other arithmetic: 71 us -> 0 us
  blocking collectives: 65 us -> 0 us
  Pallas kernels: 0 us -> 49.5 us
  matrix products: 25.5 us -> 0 us
  between operations: 21.3 us -> 2.43 us
  starting transfers between devices: 10.8 us -> 0 us
  waiting for transfers between devices: 9.86 us -> 0 us
    psum x1 -> x0, blocking collectives: 65 us -> none  [on_device(): totals = lax.psum(locals_all, ('lon', 'lat'))]
    pallas_call x0 -> x1, Pallas kernels: none -> 49.5 us  [on_device(): call(flat(conv_out), flat(cotangent), flat(field_in), kernel, line(ln_gai...]
    reduce_sum x16 -> x0, other arithmetic: 42.2 us -> none  [the longest x3 18.4 us: on_device(): jnp.sum(inner * weighted[3 + lat_off:3 + lat_off + rows, 3 + lon_off:3 +...]
    dot_general x6 -> x0, matrix products: 25.5 us -> none  [the longest x2 12.1 us: contract_last(): lax.dot_general(left, right, (((1,), (1,)), ((), ())), preferred_element_...]
    convert_element_type x4 -> x0, other arithmetic: 23.2 us -> none  [the longest x1 19.6 us: on_device(): (cotangent.astype(jnp.float32) + row_cos[:, None, None] * conv_sum).astyp...]
    ppermute x4 -> x0, starting transfers between devices: 10.7 us -> none  [the longest x2 5.67 us: extended(): after = lax.ppermute(leading, axis, down)]
    unnamed x28, local copies, waits for them, and re-layouts: 0.07 us -> 7.76 us
    psum x1 -> x0, waiting for transfers between devices: 5.56 us -> none  [on_device(): totals = lax.psum(locals_all, ('lon', 'lat'))]
  transfers between devices with their start and end apart: 5 -> 0, of which waited for: 3 -> 0; matrix products, arithmetic and copies ran while one was open for 33% -> 0% of each run, Pallas kernels for 0% -> 0%
where the time goes in v1:
time: 59.8 us; the launch traced here: 59.6 us
  Pallas kernels  49.5 us (83%)
  local copies, waits for them, and re-layouts  7.76 us (13%)
  between operations  2.43 us (4%)
    pallas_call x1, Pallas kernels, on_device(): call(flat(conv_out), flat(cotangent), flat(field_in), kernel, line(ln_gai...  49.5 us
    unnamed x28, local copies, waits for them, and re-layouts  7.76 us

profile of v1, /device:TPU:1, one launch (start us, length us, event | category | flops | bytes accessed | tf_op | source)
XLA Modules:
  0.0 59.6 jit_solution(11509996082495082957)
XLA Ops:
  0.6 49.5 %block_backward.1 = (bf16[5376,128]{1,0:T(8,128)(2,1)}, f32[49,128]{1,0:T(8,128)}, f32[1,128]{1,0:T(1,128)}, f32[1,128]{1,0:T(1,128)}, f32[1,128]{1,0:T(1,128)},...) custom-call(bf16[5376,128]{1,0:T(8,128)(2,1)} %bitcast.18, ...), custom_call_target="tpu_custom_call" | custom-call | flops 6000000000 | bytes 6000000 | tf_op jit(solution)/shard_map/block_backward/pallas_call | solution.py:543
  50.1 0.0 copy-start.2
  50.1 0.0 copy-start.8
  50.1 0.0 copy-start.7
  50.1 0.0 copy-start.6
  50.1 0.0 copy-start.1
  50.2 0.0 copy-start.3
  50.2 0.0 copy-start
  50.2 0.0 copy-start.5
  50.2 0.0 copy-start.4
  50.2 2.6 %copy.39 = bf16[96,56,128]{2,1,0:T(8,128)(2,1)} copy(bf16[96,56,128]{2,1,0:T(8,128)(2,1)} %bitcast.16) | data formatting | bytes 2752512
  52.8 0.0 copy-done.2
  52.8 0.6 %copy.40 = f32[49,128]{1,0:T(8,128)} copy(f32[49,128]{1,0:T(8,128)S(1)} %copy-done.2) | data formatting | bytes 50176
  53.4 0.0 copy-done.8
  53.4 0.5 copy.41
  53.9 0.0 copy-done.7
  53.9 0.5 copy.42
  54.4 0.0 copy-done.6
  54.4 0.5 copy.43
  54.9 0.0 copy-done.1
  54.9 0.7 %copy.44 = f32[128,512]{1,0:T(8,128)} copy(f32[128,512]{1,0:T(8,128)S(1)} %copy-done.1) | data formatting | bytes 524288
  55.6 0.0 copy-done.3
  55.6 0.6 copy.45
  56.2 0.0 copy-done
  56.2 0.7 %copy.46 = f32[512,128]{1,0:T(8,128)} copy(f32[512,128]{1,0:T(8,128)S(1)} %copy-done) | data formatting | bytes 524288
  56.9 0.0 copy-done.5
  56.9 0.5 copy.47
  57.4 0.0 copy-done.4
  57.4 0.5 copy.48
Async XLA Ops:
  50.1 2.7 %copy-start.2 = (f32[49,128]{1,0:T(8,128)S(1)}, f32[49,128]{1,0:T(8,128)}, u32[]{:S(2)}) copy-start(f32[49,128]{1,0:T(8,128)} %get-tuple-element.45) | copy-start | bytes 75268
  50.1 3.3 %copy-start.8 = (f32[1,128]{1,0:T(1,128)S(1)}, f32[1,128]{1,0:T(1,128)}, u32[]{:S(2)}) copy-start(f32[1,128]{1,0:T(1,128)} %get-tuple-element.24) | copy-start | bytes 1540
  50.1 3.8 %copy-start.7 = (f32[1,128]{1,0:T(1,128)S(1)}, f32[1,128]{1,0:T(1,128)}, u32[]{:S(2)}) copy-start(f32[1,128]{1,0:T(1,128)} %get-tuple-element.25) | copy-start | bytes 1540
  50.1 4.3 %copy-start.6 = (f32[1,128]{1,0:T(1,128)S(1)}, f32[1,128]{1,0:T(1,128)}, u32[]{:S(2)}) copy-start(f32[1,128]{1,0:T(1,128)} %get-tuple-element.26) | copy-start | bytes 1540
  50.1 4.8 %copy-start.1 = (f32[128,512]{1,0:T(8,128)S(1)}, f32[128,512]{1,0:T(8,128)}, u32[]{:S(2)}) copy-start(f32[128,512]{1,0:T(8,128)} %get-tuple-element.49) | copy-start | bytes 786436
  50.2 5.5 %copy-start.3 = (f32[1,512]{1,0:T(1,128)S(1)}, f32[1,512]{1,0:T(1,128)}, u32[]{:S(2)}) copy-start(f32[1,512]{1,0:T(1,128)} %get-tuple-element.28) | copy-start | bytes 6148
  50.2 6.1 %copy-start = (f32[512,128]{1,0:T(8,128)S(1)}, f32[512,128]{1,0:T(8,128)}, u32[]{:S(2)}) copy-start(f32[512,128]{1,0:T(8,128)} %get-tuple-element.51) | copy-start | bytes 786436
  50.2 6.7 %copy-start.5 = (f32[1,128]{1,0:T(1,128)S(1)}, f32[1,128]{1,0:T(1,128)}, u32[]{:S(2)}) copy-start(f32[1,128]{1,0:T(1,128)} %get-tuple-element.30) | copy-start | bytes 1540
  50.2 7.3 %copy-start.4 = (f32[1,128]{1,0:T(1,128)S(1)}, f32[1,128]{1,0:T(1,128)}, u32[]{:S(2)}) copy-start(f32[1,128]{1,0:T(1,128)} %get-tuple-element.31) | copy-start | bytes 1540

commit v2 on v1

v2 whole, which is shorter than its diff:
```python
import math

import jax
import jax.numpy as jnp
import ml_dtypes
import numpy as np
from jax import lax
from jax.experimental import pallas as pl
from jax.experimental.pallas import tpu as pltpu
from jax.sharding import PartitionSpec as P

MESH = pl.DeviceIdType.MESH
f32, bf16 = jnp.float32, jnp.bfloat16
EPS = 1e-06
COEF = 0.044715
ROOT = math.sqrt(2.0 / math.pi)

N = 14
OUT = 8
PAIRS = 104
FREQ = 2 * PAIRS
SCALE = 1.828125
LAT_ROWS, COLS, CH, HID, TAPS = 96, 56, 128, 512, 49
TL, TC = LAT_ROWS // OUT, COLS // OUT
SMALL = 64
RIM = ((0, 0, LAT_ROWS), (TC - 1, 0, LAT_ROWS))


def tables():
    own = [(0, 0), (0, 7), (7, 0), (7, 7)]
    seen, pairs = set(own), []
    for k in range(N):
        for l in range(N):
            if (k, l) not in seen:
                seen.add((k, l))
                seen.add(((-k) % N, (-l) % N))
                pairs.append((k, l))
    freq = np.array(own + pairs)
    weight = np.array([1.0] * 4 + [2.0] * 96)[:, None] / (N * N)
    twin = np.array([0.0] * 4 + [1.0] * 96)[:, None]

    def angle(rows, cols, row_off, col_off):
        m, n = np.meshgrid(np.arange(rows) + row_off, np.arange(cols) + col_off, indexing="ij")
        m, n = m.ravel(), n.ravel()
        return 2 * np.pi * ((np.outer(freq[:, 0], m) + np.outer(freq[:, 1], n)) % N) / N

    def interleave(re, im):
        fill = np.zeros((PAIRS - 100, re.shape[1]))
        re, im = np.concatenate([re, fill]), np.concatenate([im, fill])
        shape = (PAIRS // 8, 8, re.shape[1])
        return np.stack([re.reshape(shape), im.reshape(shape)], 1).reshape(FREQ, -1)

    inside = np.tile(np.array([0.0] + [1.0] * 14 + [0.0]), N)
    a = angle(N, 16, 0, -1)
    fwd = interleave(np.cos(a) * inside, -np.sin(a) * inside * twin)
    a = angle(OUT, OUT, 6, 6)
    fwd_tile = interleave(np.cos(a), -np.sin(a) * twin)
    inv = interleave(np.cos(a) * weight, -np.sin(a) * weight * twin).T
    a = angle(7, 7, 0, 0)
    taps = interleave(np.cos(a), -np.sin(a) * twin)
    taps_inv = interleave(np.cos(a) * weight, -np.sin(a) * weight * twin).T
    area = N * N
    return (
        (fwd * SCALE).astype(ml_dtypes.bfloat16),
        (fwd_tile * SCALE).astype(ml_dtypes.bfloat16),
        (inv * area * SCALE).astype(ml_dtypes.bfloat16),
        (np.pad(taps, ((0, 0), (0, 7))) / (area * SCALE * SCALE)).astype(np.float32),
        (np.pad(taps_inv, ((0, 7), (0, 0))) / (SCALE * SCALE)).astype(np.float32),
    )


def dot(a, b):
    return jnp.dot(a, b, preferred_element_type=f32)


def dot_exact(a, b):
    return jnp.dot(a, b, preferred_element_type=f32, precision=lax.Precision.HIGHEST)


def dot_last(a, b):
    return lax.dot_general(a, b, (((1,), (1,)), ((), ())), preferred_element_type=f32)


def dot_rows(a, b):
    return lax.dot_general(a, b, (((0,), (0,)), ((), ())), preferred_element_type=f32)


def rows8(v):
    return jnp.sum(v.reshape(v.shape[0] // 8, 8, v.shape[1]), 0)


def make_kernel(nz, nx, nyh, nyl, ncore, total_cells):
    nlon, nlat = nz * nx * nyh, nyl * ncore
    ny = nyh * nyl
    nb, na = nz * ny, nx * ncore
    wrows = 2 * CH // nb
    srows = SMALL // na
    factor = float(total_cells) ** (-0.5)

    def kernel(
        x_hbm, c_hbm, f_hbm, ker_hbm, gain_ref, bias_ref, win_ref, bin_ref, wout_ref, bout_ref, ls_ref,
        cos_ref, mf_hbm, mg_hbm, mi_hbm, mk_hbm, md_hbm,
        out_hbm, dk_ref, dcb_ref, dgain_ref, dbias_ref, dwin_ref, dbin_ref, dwout_ref, dbout_ref, dls_ref, norm_ref,
        xv, cv, fv, outv, dup, yb, mf, mg, mi, mk, md, ker, kpad, kh, acc, gw, gbin, small, sm32,
        hs, hr, vs, vr, ws, wr, w2, wf, s0, s1, s2, s3,
        in_sem, const_sem, out_sem, h_send, h_recv, v_send, v_recv,
        w1_send, w1_recv, w2_send, w2_recv, w3_send, w3_recv, s1_send, s1_recv, s2_send, s2_recv, s3_send, s3_recv,
    ):
        lon, lat = lax.axis_index("lon"), lax.axis_index("lat")
        z, x, yh = lax.div(lon, nx * nyh), lax.rem(lax.div(lon, nyh), nx), lax.rem(lon, nyh)
        yl, core = lax.div(lat, ncore), lax.rem(lat, ncore)
        b_me = z * ny + yh * nyl + yl
        a_me = x * ncore + core

        def b_peer(b):
            bz, by = lax.div(b, ny), lax.rem(b, ny)
            return (bz * (nx * nyh) + x * nyh + lax.div(by, nyl), lax.rem(by, nyl) * ncore + core)

        def a_peer(a):
            return (z * (nx * nyh) + lax.div(a, ncore) * nyh + yh, yl * ncore + lax.rem(a, ncore))

        right, left = lax.rem(lon + 1, nlon), lax.rem(lon + nlon - 1, nlon)
        down, up = lax.rem(lat + 1, nlat), lax.rem(lat + nlat - 1, nlat)

        def load(which, t):
            src, dst = ((x_hbm, xv), (c_hbm, cv), (f_hbm, fv))[which]
            return pltpu.make_async_copy(src.at[:, pl.ds(8 * t, 8), :], dst.at[t], in_sem.at[which, t])

        consts = ((mf_hbm, mf), (mg_hbm, mg), (mk_hbm, mk), (ker_hbm, ker), (md_hbm, md), (mi_hbm, mi))

        def load_const(i):
            return pltpu.make_async_copy(*consts[i], const_sem.at[i])

        for t in (0, TC - 1, *range(1, TC - 1)):
            load(0, t).start()
            load(1, t).start()
        for i in range(len(consts)):
            load_const(i).start()
        for t in range(TC):
            load(2, t).start()

        barrier = pltpu.get_barrier_semaphore()
        for peer in ((right, lat), (left, lat), (lon, down), (lon, up)):
            pl.semaphore_signal(barrier, inc=1, device_id=peer, device_id_type=MESH)

        def greet_b(d, carry):
            pl.semaphore_signal(barrier, inc=1, device_id=b_peer(lax.rem(b_me + d, nb)), device_id_type=MESH)
            return carry

        def greet_a(d, carry):
            pl.semaphore_signal(barrier, inc=1, device_id=a_peer(lax.rem(a_me + d, na)), device_id_type=MESH)
            return carry

        lax.fori_loop(1, nb, greet_b, 0)
        lax.fori_loop(1, na, greet_a, 0)

        third = jnp.full((CH, CH), 1.0 / CH, bf16)
        none = jnp.zeros((CH, CH), bf16)
        mean_two = jnp.concatenate(
            [jnp.concatenate([third, none], 1), jnp.concatenate([none, third], 1)], 0
        )
        gain, bias, scale = gain_ref[...], bias_ref[...], ls_ref[...]
        gw[...] = jnp.zeros_like(gw)
        gbin[...] = jnp.zeros_like(gbin)
        small[...] = jnp.zeros_like(small)
        acc[...] = jnp.zeros_like(acc)
        kpad[...] = jnp.zeros_like(kpad)

        def mlp(parts):
            def cells_of(ref):
                return jnp.concatenate(
                    [ref[t, pl.ds(r0, n)].astype(f32).reshape(n * 8, CH) for t, r0, n in parts], 0
                )

            value = cells_of(xv)
            center = value - dot(value.astype(bf16), third)
            rstd = lax.rsqrt(dot((center * center).astype(bf16), third) + EPS)
            normed = center * rstd
            zed = (normed * gain + bias).astype(bf16)
            cot = cells_of(cv)
            cb = cot.astype(bf16)
            d_out = (cot * scale).astype(bf16)
            acts, dpres = [], []
            g_bin = jnp.zeros((8, HID), f32)
            sub = value.shape[0] // 2
            for s in range(0, value.shape[0], sub):
                h = dot(zed[s : s + sub], win_ref[...]) + bin_ref[...]
                d_act = dot_last(d_out[s : s + sub], wout_ref[...])
                h2 = h * h
                inner = h * (ROOT + (ROOT * COEF) * h2)
                wide = h * (2 * ROOT + (6 * ROOT * COEF) * h2)
                gate = 0.5 * jnp.tanh(inner) + 0.5
                d_pre = d_act * (gate * (1.0 + (1.0 - gate) * wide))
                g_bin = g_bin + rows8(d_pre)
                acts.append((h * gate).astype(bf16))
                dpres.append(d_pre.astype(bf16))
            act, d_pre = jnp.concatenate(acts, 0), jnp.concatenate(dpres, 0)
            gbin[...] += g_bin
            gw[CH:, :] += dot_rows(cb, act)
            gw[:CH, :] += dot_rows(zed, d_pre)
            d_zed = dot_last(d_pre, win_ref[...])
            d_gain = d_zed * normed
            d_norm = d_zed * gain
            means = dot(
                jnp.concatenate([d_norm.astype(bf16), (d_gain * gain).astype(bf16)], 1), mean_two
            )
            du = rstd * (d_norm - means[:, :CH] - normed * means[:, CH:])
            at = 0
            for t, r0, n in parts:
                dup[pl.ds(3 + r0, n), 4 + 8 * t : 12 + 8 * t, :] = du[at : at + 8 * n].reshape(n, 8, CH)
                at += 8 * n
            small[0] += rows8(d_gain)
            small[1] += rows8(d_zed)
            small[2] += rows8(du)
            small[3] += rows8(cot)

        for t in (0, TC - 1):
            load(0, t).wait()
            load(1, t).wait()
        mlp(RIM)

        half = LAT_ROWS // 2
        low = lax.broadcasted_iota(jnp.int32, (half, 8, CH), 1) < 4

        def copy_h(side):
            return pltpu.make_async_remote_copy(
                src_ref=hs.at[side], dst_ref=hr.at[side], send_sem=h_send.at[side], recv_sem=h_recv.at[side],
                device_id=((right, lat), (left, lat))[side], device_id_type=MESH,
            )

        def copy_v(side):
            return pltpu.make_async_remote_copy(
                src_ref=vs.at[side], dst_ref=vr.at[side], send_sem=v_send.at[side], recv_sem=v_recv.at[side],
                device_id=((lon, down), (lon, up))[side], device_id_type=MESH,
            )

        pl.semaphore_wait(barrier, 4 + (nb - 1) + (na - 1))
        first, second = dup[3 : 3 + half, 56:64, :], dup[3 + half : 3 + LAT_ROWS, 56:64, :]
        hs[0] = jnp.where(low, first, pltpu.roll(second, 4, 1)).reshape(half * 8, CH).astype(bf16)
        copy_h(0).start()
        first, second = dup[3 : 3 + half, 0:8, :], dup[3 + half : 3 + LAT_ROWS, 0:8, :]
        hs[1] = jnp.where(low, pltpu.roll(second, 4, 1), first).reshape(half * 8, CH).astype(bf16)
        copy_h(1).start()

        for t in range(1, TC - 1):
            load(0, t).wait()
            load(1, t).wait()

        def mlp_middle(i, carry):
            mlp([(t, i * half, half) for t in range(1, TC - 1)])
            return carry

        lax.fori_loop(0, 2, mlp_middle, 0)

        def copy_w1(b_to, b_from):
            return pltpu.make_async_remote_copy(
                src_ref=ws.at[b_to], dst_ref=wr.at[b_from], send_sem=w1_send.at[b_to], recv_sem=w1_recv.at[b_from],
                device_id=b_peer(b_to), device_id_type=MESH,
            )

        def copy_w2(a_to, a_from):
            return pltpu.make_async_remote_copy(
                src_ref=w2.at[a_me], dst_ref=w2.at[a_from], send_sem=w2_send.at[a_to], recv_sem=w2_recv.at[a_from],
                device_id=a_peer(a_to), device_id_type=MESH,
            )

        def copy_w3(b_to, b_from):
            return pltpu.make_async_remote_copy(
                src_ref=wf.at[b_me], dst_ref=wf.at[b_from], send_sem=w3_send.at[b_to], recv_sem=w3_recv.at[b_from],
                device_id=b_peer(b_to), device_id_type=MESH,
            )

        def copy_s1(a_to, a_from):
            return pltpu.make_async_remote_copy(
                src_ref=s0.at[a_to], dst_ref=s1.at[a_from], send_sem=s1_send.at[a_to], recv_sem=s1_recv.at[a_from],
                device_id=a_peer(a_to), device_id_type=MESH,
            )

        def copy_s2(b_to, b_from):
            return pltpu.make_async_remote_copy(
                src_ref=s2.at[b_me], dst_ref=s2.at[b_from], send_sem=s2_send.at[b_to], recv_sem=s2_recv.at[b_from],
                device_id=b_peer(b_to), device_id_type=MESH,
            )

        def copy_s3(a_to, a_from):
            return pltpu.make_async_remote_copy(
                src_ref=s3.at[a_me], dst_ref=s3.at[a_from], send_sem=s3_send.at[a_to], recv_sem=s3_recv.at[a_from],
                device_id=a_peer(a_to), device_id_type=MESH,
            )

        def over(copy, act, me, size):
            def body(d, carry):
                peer = lax.rem(me + d, size)
                if act == "send":
                    copy(peer, me).start()
                elif act == "recv":
                    copy(peer, peer).wait_recv()
                else:
                    copy(peer, me).wait_send()
                return carry

            lax.fori_loop(1, size, body, 0)

        def over_a(copy, act):
            over(copy, act, a_me, na)

        def over_b(copy, act):
            over(copy, act, b_me, nb)

        ws[...] = gw[...].astype(bf16).reshape(nb, wrows, HID)
        over_b(copy_w1, "send")

        copy_h(0).wait_recv()
        copy_h(1).wait_recv()
        near = hr[0].astype(f32).reshape(half, 8, CH)
        dup[3 : 3 + half, 0:8, :] = jnp.where(low, near, dup[3 : 3 + half, 0:8, :])
        dup[3 + half : 3 + LAT_ROWS, 0:8, :] = jnp.where(
            low, pltpu.roll(near, 4, 1), dup[3 + half : 3 + LAT_ROWS, 0:8, :]
        )
        near = hr[1].astype(f32).reshape(half, 8, CH)
        dup[3 : 3 + half, 56:64, :] = jnp.where(low, dup[3 : 3 + half, 56:64, :], near)
        dup[3 + half : 3 + LAT_ROWS, 56:64, :] = jnp.where(
            low, dup[3 + half : 3 + LAT_ROWS, 56:64, :], pltpu.roll(near, 4, 1)
        )
        vs[0] = dup[LAT_ROWS : LAT_ROWS + 3].reshape(192, CH).astype(bf16)
        vs[1] = dup[3:6].reshape(192, CH).astype(bf16)
        copy_v(0).start()
        copy_v(1).start()

        for i in range(len(consts)):
            load_const(i).wait()
        for t in range(TC):
            load(2, t).wait()
        kpad[0:TAPS] = ker[...]
        kh[...] = dot_exact(mk[...], kpad[...])

        def tile_pair(slot, i0, i1, t):
            def window(i):
                return dup[pl.ds(i * OUT, N), 8 * t : 8 * t + 16, :].reshape(N * 16, CH).astype(bf16)

            def field(i):
                tile = fv[t, pl.ds(i * OUT, OUT)].astype(f32)
                tile = [tile[r] * cos_ref[lat * LAT_ROWS + i * OUT + r] for r in range(OUT)]
                return jnp.concatenate(tile, 0).astype(bf16)

            shape = (PAIRS // 8, 2, 8, 2 * CH)
            w = dot(mf[...], jnp.concatenate([window(i0), window(i1)], 1)).reshape(shape)
            g = dot(mg[...], jnp.concatenate([field(i0), field(i1)], 1)).reshape(shape)
            k = kh[...].reshape(PAIRS // 8, 2, 8, CH)
            k = jnp.concatenate([k, k], -1)
            w_re, w_im, g_re, g_im, k_re, k_im = w[:, 0], w[:, 1], g[:, 0], g[:, 1], k[:, 0], k[:, 1]
            y = jnp.stack([k_re * w_re - k_im * w_im, k_re * w_im + k_im * w_re], 1)
            yb[slot] = y.reshape(FREQ, 2 * CH).astype(bf16)
            d = jnp.stack([g_re * w_re + g_im * w_im, g_im * w_re - g_re * w_im], 1).reshape(FREQ, 2 * CH)
            acc[...] += d[:, :CH] + d[:, CH:]

        pairs = TL // 2

        def middle(j, carry):
            for t in range(1, TC - 1):
                tile_pair(t * pairs + j, 1 + 2 * j, 2 + 2 * j, t)
            return carry

        def sides(j, carry):
            for t in (0, TC - 1):
                tile_pair(t * pairs + j, 1 + 2 * j, 2 + 2 * j, t)
            return carry

        lax.fori_loop(0, pairs - 1, middle, 0)
        lax.fori_loop(0, pairs - 1, sides, 0)

        wr[b_me] = ws[b_me]
        over_b(copy_w1, "recv")
        w2[a_me] = jnp.sum(wr[...].astype(f32), 0).astype(bf16)
        over_a(copy_w2, "send")

        copy_v(0).wait_recv()
        copy_v(1).wait_recv()
        zero = jnp.zeros((3, 64, CH), f32)
        dup[0:3] = jnp.where(lat > 0, vr[0].astype(f32).reshape(3, 64, CH), zero)
        dup[LAT_ROWS + 3 : LAT_ROWS + 6] = jnp.where(lat < nlat - 1, vr[1].astype(f32).reshape(3, 64, CH), zero)
        for t in range(TC):
            tile_pair(t * pairs + pairs - 1, 0, TL - 1, t)

        sm32[...] = jnp.zeros_like(sm32)
        sm32[0:56] = dot_exact(md[...], acc[...])
        total = jnp.sum(gbin[...], 0, keepdims=True)
        for q in range(4):
            sm32[49 + q : 50 + q] = total[:, q * CH : (q + 1) * CH]
            sm32[53 + q : 54 + q] = jnp.sum(small[q], 0, keepdims=True)
        s0[...] = sm32[...].reshape(na, srows, CH)
        over_a(copy_s1, "send")

        def store(t):
            return pltpu.make_async_copy(outv.at[t], out_hbm.at[:, pl.ds(8 * t, 8), :], out_sem.at[t])

        def finish(t, carry):
            for j in range(pairs):
                conv = dot(mi[...], yb[t * pairs + j]).reshape(OUT, OUT, 2 * CH)
                ends = (0, TL - 1) if j == pairs - 1 else (1 + 2 * j, 2 + 2 * j)
                for n, i in enumerate(ends):
                    cot = cv[t, i * OUT : (i + 1) * OUT].astype(f32)
                    part = conv[:, :, n * CH : (n + 1) * CH]
                    value = [cot[r] + part[r] * cos_ref[lat * LAT_ROWS + i * OUT + r] for r in range(OUT)]
                    outv[t, i * OUT : (i + 1) * OUT] = jnp.stack(value, 0).astype(bf16)
            store(t).start()
            return carry

        lax.fori_loop(0, 4, finish, 0)
        s1[a_me] = s0[a_me]
        over_a(copy_s1, "recv")
        s2[b_me] = jnp.sum(s1[...], 0)
        over_b(copy_s2, "send")
        over_a(copy_w2, "recv")
        wf[b_me] = jnp.sum(w2[...].astype(f32), 0).astype(bf16)
        over_b(copy_w3, "send")
        lax.fori_loop(4, TC, finish, 0)
        over_b(copy_s2, "recv")
        s3[a_me] = jnp.sum(s2[...], 0)
        over_a(copy_s3, "send")

        over_b(copy_w3, "recv")
        d_win = jnp.concatenate([wf[b].astype(f32) for b in range(nb // 2)], 0) * factor
        dwin_ref[...] = d_win
        g_out = jnp.concatenate([wf[b].astype(f32) for b in range(nb // 2, nb)], 0) * factor
        g_out = g_out.T
        d_wout = g_out * scale
        dwout_ref[...] = d_wout
        over_a(copy_s3, "recv")
        sm32[...] = s3[...].reshape(SMALL, CH) * factor
        dk = sm32[0:TAPS]
        d_bin = jnp.concatenate([sm32[49 + q : 50 + q] for q in range(4)], 1)
        d_gain, d_bias, d_cb, s_cot = (sm32[53 + q : 54 + q] for q in range(4))
        d_bout = s_cot * scale
        d_ls = jnp.sum(g_out * wout_ref[...].astype(f32), 0, keepdims=True) + bout_ref[...] * s_cot
        dk_ref[...] = dk
        dbin_ref[...] = d_bin
        dgain_ref[...] = d_gain
        dbias_ref[...] = d_bias
        dcb_ref[...] = d_cb
        dbout_ref[...] = d_bout
        dls_ref[...] = d_ls
        squares = jnp.sum(d_win * d_win, 0, keepdims=True) + d_bin * d_bin
        squares = sum(squares[:, q * CH : (q + 1) * CH] for q in range(4))
        squares = squares + jnp.sum(d_wout * d_wout, 0, keepdims=True) + jnp.sum(dk * dk, 0, keepdims=True)
        for part in (d_gain, d_bias, d_cb, d_bout, d_ls):
            squares = squares + part * part
        norm_ref[...] = jnp.sqrt(jnp.sum(squares, 1, keepdims=True))

        for side in range(2):
            copy_h(side).wait_send()
            copy_v(side).wait_send()
        over_b(copy_w1, "done")
        over_a(copy_w2, "done")
        over_b(copy_w3, "done")
        over_a(copy_s1, "done")
        over_b(copy_s2, "done")
        over_a(copy_s3, "done")
        for t in range(TC):
            store(t).wait()

    hbm, vmem, smem = (pl.BlockSpec(memory_space=m) for m in (pl.ANY, pltpu.VMEM, pltpu.SMEM))
    shape = jax.ShapeDtypeStruct
    dma = pltpu.SemaphoreType.DMA
    by_tile = (TC, LAT_ROWS, 8, CH)
    return pl.pallas_call(
        kernel,
        in_specs=[hbm] * 4 + [vmem] * 7 + [smem] + [hbm] * 5,
        out_specs=[hbm] + [vmem] * 10,
        out_shape=RESULTS,
        scratch_shapes=[
            pltpu.VMEM(by_tile, bf16),
            pltpu.VMEM(by_tile, bf16),
            pltpu.VMEM(by_tile, bf16),
            pltpu.VMEM(by_tile, bf16),
            pltpu.VMEM((LAT_ROWS + 6, COLS + 8, CH), f32),
            pltpu.VMEM((TL * TC // 2, FREQ, 2 * CH), bf16),
            pltpu.VMEM((FREQ, N * 16), bf16),
            pltpu.VMEM((FREQ, OUT * OUT), bf16),
            pltpu.VMEM((OUT * OUT, FREQ), bf16),
            pltpu.VMEM((FREQ, 56), f32),
            pltpu.VMEM((56, FREQ), f32),
            pltpu.VMEM((TAPS, CH), f32),
            pltpu.VMEM((56, CH), f32),
            pltpu.VMEM((FREQ, CH), f32),
            pltpu.VMEM((FREQ, CH), f32),
            pltpu.VMEM((2 * CH, HID), f32),
            pltpu.VMEM((8, HID), f32),
            pltpu.VMEM((4, 8, CH), f32),
            pltpu.VMEM((SMALL, CH), f32),
            pltpu.VMEM((2, LAT_ROWS * 4, CH), bf16),
            pltpu.VMEM((2, LAT_ROWS * 4, CH), bf16),
            pltpu.VMEM((2, 192, CH), bf16),
            pltpu.VMEM((2, 192, CH), bf16),
            pltpu.VMEM((nb, wrows, HID), bf16),
            pltpu.VMEM((nb, wrows, HID), bf16),
            pltpu.VMEM((na, wrows, HID), bf16),
            pltpu.VMEM((nb, wrows, HID), bf16),
            pltpu.VMEM((na, srows, CH), f32),
            pltpu.VMEM((na, srows, CH), f32),
            pltpu.VMEM((nb, srows, CH), f32),
            pltpu.VMEM((na, srows, CH), f32),
            dma((3, TC)),
            dma((6,)),
            dma((TC,)),
            dma((2,)),
            dma((2,)),
            dma((2,)),
            dma((2,)),
        ]
        + [dma((n,)) for n in (nb, nb, na, na, nb, nb, na, na, nb, nb, na, na)],
        compiler_params=pltpu.CompilerParams(
            collective_id=0, has_side_effects=True, vmem_limit_bytes=60 * 2**20
        ),
        cost_estimate=pl.CostEstimate(flops=6 * 10**9, bytes_accessed=6 * 10**6, transcendentals=3 * 10**6),
        name="block_backward",
    )


RESULTS = [
    jax.ShapeDtypeStruct(s, t)
    for s, t in (
        ((LAT_ROWS, COLS, CH), bf16),
        ((TAPS, CH), f32),
        ((1, CH), f32),
        ((1, CH), f32),
        ((1, CH), f32),
        ((CH, HID), f32),
        ((1, HID), f32),
        ((HID, CH), f32),
        ((1, CH), f32),
        ((1, CH), f32),
        ((1, 1), f32),
    )
]
BANDS = 6


def hand_on(*refs):
    n = len(RESULTS)
    src, dst, sem = refs[:n], refs[n : 2 * n], refs[2 * n]
    rows = LAT_ROWS // BANDS
    copies = [
        pltpu.make_async_copy(src[0].at[pl.ds(i * rows, rows)], dst[0].at[pl.ds(i * rows, rows)], sem.at[n + i])
        for i in range(BANDS)
    ]
    copies += [pltpu.make_async_copy(src[i], dst[i], sem.at[i]) for i in range(1, n)]
    for copy in copies:
        copy.start()
    for copy in copies:
        copy.wait()


def make_hand_on():
    n = len(RESULTS)
    hbm = pl.BlockSpec(memory_space=pl.ANY)
    return pl.pallas_call(
        hand_on,
        in_specs=[hbm] * n,
        out_specs=[hbm] * n,
        out_shape=RESULTS,
        scratch_shapes=[pltpu.SemaphoreType.DMA((n + BANDS,))],
        name="hand_on",
    )


def solution(mesh):
    nlon, nlat = mesh.shape["lon"], mesh.shape["lat"]
    nz, nx, nyh = (4, 4, 2) if nlon == 32 else (nlon, 1, 1)
    nyl, ncore = nlat // 2, 2
    total_rows, total_cols = LAT_ROWS * nlat, COLS * nlon
    call = make_kernel(nz, nx, nyh, nyl, ncore, total_rows * total_cols)
    finish = make_hand_on()
    fwd, fwd_tile, inv, taps, taps_inv = tables()
    place = (np.arange(total_rows, dtype=np.float32) + np.float32(0.5)) / np.float32(total_rows) - np.float32(0.5)
    weight = np.cos(np.float32(math.pi) * place).astype(np.float32)

    def on_device(field_in, conv_out, cotangent, kernel, ln_gain, ln_bias, w_in, b_in, w_out, b_out, layer_scale):
        line = lambda v: v.reshape(1, -1)
        outs = call(
            conv_out, cotangent, field_in, kernel, line(ln_gain), line(ln_bias), w_in, line(b_in),
            w_out, line(b_out), line(layer_scale), weight, fwd, fwd_tile, inv, taps, taps_inv,
        )
        d_field, d_kernel, d_cb, d_gain, d_bias, d_win, d_bin, d_wout, d_bout, d_ls, norm = finish(*outs)
        wide = lambda v: v.reshape(-1)
        return (
            d_field, d_kernel, wide(d_cb), wide(d_gain), wide(d_bias), d_win, wide(d_bin),
            d_wout, wide(d_bout), wide(d_ls), norm.reshape(()),
        )

    grid = P("lat", "lon", None)
    return jax.shard_map(
        on_device,
        mesh=mesh,
        in_specs=(grid, grid, grid) + (P(),) * 8,
        out_specs=(grid,) + (P(),) * 10,
        check_vma=False,
    )
```

time: 59.8 us -> 106 us (1.77)
  Pallas kernels: 49.5 us -> 105 us
  local copies, waits for them, and re-layouts: 7.76 us -> 0 us
  between operations: 2.43 us -> 0.66 us
    pallas_call x1 -> x2, Pallas kernels: 49.5 us -> 105 us  [the longest x1 60.4 us: on_device(): finish(*outs)]
    unnamed x28 -> x0, local copies, waits for them, and re-layouts: 7.76 us -> none
where the time goes in v2:
time: 106 us
  Pallas kernels  105 us (99%)
    pallas_call x1, Pallas kernels, on_device(): finish(*outs)  60.4 us
    pallas_call x1, Pallas kernels, on_device(): call(conv_out, cotangent, field_in, kernel, line(ln_gain), line(ln_bias),...  44.6 us

profile of v2, /device:TPU:1, one launch (start us, length us, event | category | flops | bytes accessed | tf_op | source)
XLA Modules:
  0.0 105.6 jit_solution(2379166191894865728)
XLA Ops:
  0.6 44.6 %block_backward.1 = (bf16[96,56,128]{2,1,0:T(8,128)(2,1)}, f32[49,128]{1,0:T(8,128)}, f32[1,128]{1,0:T(1,128)}, f32[1,128]{1,0:T(1,128)}, f32[1,128]{1,0:T(1,128...) custom-call(bf16[96,56,128]{2,1,0:T(8,128)(2,1)} %x_hbm.1, ...), custom_call_target="tpu_custom_call" | custom-call | flops 6000000000 | bytes 6000000 | tf_op jit(solution)/shard_map/block_backward/pallas_call | solution.py:580
  45.2 60.4 %hand_on.1 = (bf16[96,56,128]{2,1,0:T(8,128)(2,1)}, f32[49,128]{1,0:T(8,128)}, f32[1,128]{1,0:T(1,128)}, f32[1,128]{1,0:T(1,128)}, f32[1,128]{1,0:T(1,128)}, /*i...) custom-call(bf16[96,56,128]{2,1,0:T(8,128)(2,1)} %get-tuple-element., ...), custom_call_target="tpu_custom_call" | custom-call | tf_op jit(solution)/shard_map/hand_on/pallas_call | solution.py:584

commit v3 on v2

--- a/solution.py
+++ b/solution.py
@@ -94,7 +94,6 @@
     ny = nyh * nyl
     nb, na = nz * ny, nx * ncore
     wrows = 2 * CH // nb
-    srows = SMALL // na
     factor = float(total_cells) ** (-0.5)
 
     def kernel(
@@ -102,9 +101,9 @@
         cos_ref, mf_hbm, mg_hbm, mi_hbm, mk_hbm, md_hbm,
         out_hbm, dk_ref, dcb_ref, dgain_ref, dbias_ref, dwin_ref, dbin_ref, dwout_ref, dbout_ref, dls_ref, norm_ref,
         xv, cv, fv, outv, dup, yb, mf, mg, mi, mk, md, ker, kpad, kh, acc, gw, gbin, small, sm32,
-        hs, hr, vs, vr, ws, wr, w2, wf, s0, s1, s2, s3,
+        hs, hr, vs, vr, ws, wr, w2, wf, s1, s2,
         in_sem, const_sem, out_sem, h_send, h_recv, v_send, v_recv,
-        w1_send, w1_recv, w2_send, w2_recv, w3_send, w3_recv, s1_send, s1_recv, s2_send, s2_recv, s3_send, s3_recv,
+        w1_send, w1_recv, w2_send, w2_recv, w3_send, w3_recv, s1_send, s1_recv, s2_send, s2_recv,
     ):
         lon, lat = lax.axis_index("lon"), lax.axis_index("lat")
         z, x, yh = lax.div(lon, nx * nyh), lax.rem(lax.div(lon, nyh), nx), lax.rem(lon, nyh)
@@ -272,7 +271,7 @@
 
         def copy_s1(a_to, a_from):
             return pltpu.make_async_remote_copy(
-                src_ref=s0.at[a_to], dst_ref=s1.at[a_from], send_sem=s1_send.at[a_to], recv_sem=s1_recv.at[a_from],
+                src_ref=s1.at[a_me], dst_ref=s1.at[a_from], send_sem=s1_send.at[a_to], recv_sem=s1_recv.at[a_from],
                 device_id=a_peer(a_to), device_id_type=MESH,
             )
 
@@ -280,12 +279,6 @@
             return pltpu.make_async_remote_copy(
                 src_ref=s2.at[b_me], dst_ref=s2.at[b_from], send_sem=s2_send.at[b_to], recv_sem=s2_recv.at[b_from],
                 device_id=b_peer(b_to), device_id_type=MESH,
-            )
-
-        def copy_s3(a_to, a_from):
-            return pltpu.make_async_remote_copy(
-                src_ref=s3.at[a_me], dst_ref=s3.at[a_from], send_sem=s3_send.at[a_to], recv_sem=s3_recv.at[a_from],
-                device_id=a_peer(a_to), device_id_type=MESH,
             )
 
         def over(copy, act, me, size):
@@ -369,11 +362,6 @@
         lax.fori_loop(0, pairs - 1, middle, 0)
         lax.fori_loop(0, pairs - 1, sides, 0)
 
-        wr[b_me] = ws[b_me]
-        over_b(copy_w1, "recv")
-        w2[a_me] = jnp.sum(wr[...].astype(f32), 0).astype(bf16)
-        over_a(copy_w2, "send")
-
         copy_v(0).wait_recv()
         copy_v(1).wait_recv()
         zero = jnp.zeros((3, 64, CH), f32)
@@ -388,7 +376,7 @@
         for q in range(4):
             sm32[49 + q : 50 + q] = total[:, q * CH : (q + 1) * CH]
             sm32[53 + q : 54 + q] = jnp.sum(small[q], 0, keepdims=True)
-        s0[...] = sm32[...].reshape(na, srows, CH)
+        s1[a_me] = sm32[...].astype(bf16)
         over_a(copy_s1, "send")
 
         def store(t):
@@ -406,19 +394,31 @@
             store(t).start()
             return carry
 
-        lax.fori_loop(0, 4, finish, 0)
-        s1[a_me] = s0[a_me]
+        lax.fori_loop(0, 3, finish, 0)
+        wr[b_me] = ws[b_me]
+        over_b(copy_w1, "recv")
+        w2[a_me] = jnp.sum(wr[...].astype(f32), 0).astype(bf16)
+        over_a(copy_w2, "send")
+        lax.fori_loop(3, TC, finish, 0)
         over_a(copy_s1, "recv")
-        s2[b_me] = jnp.sum(s1[...], 0)
+        s2[b_me] = jnp.sum(s1[...].astype(f32), 0).astype(bf16)
         over_b(copy_s2, "send")
         over_a(copy_w2, "recv")
         wf[b_me] = jnp.sum(w2[...].astype(f32), 0).astype(bf16)
         over_b(copy_w3, "send")
-        lax.fori_loop(4, TC, finish, 0)
+
         over_b(copy_s2, "recv")
-        s3[a_me] = jnp.sum(s2[...], 0)
-        over_a(copy_s3, "send")
-
+        sm32[...] = jnp.sum(s2[...].astype(f32), 0) * factor
+        dk = sm32[0:TAPS]
+        d_bin = jnp.concatenate([sm32[49 + q : 50 + q] for q in range(4)], 1)
+        d_gain, d_bias, d_cb, s_cot = (sm32[53 + q : 54 + q] for q in range(4))
+        d_bout = s_cot * scale
+        dk_ref[...] = dk
+        dbin_ref[...] = d_bin
+        dgain_ref[...] = d_gain
+        dbias_ref[...] = d_bias
+        dcb_ref[...] = d_cb
+        dbout_ref[...] = d_bout
         over_b(copy_w3, "recv")
         d_win = jnp.concatenate([wf[b].astype(f32) for b in range(nb // 2)], 0) * factor
         dwin_ref[...] = d_win
@@ -426,19 +426,7 @@
         g_out = g_out.T
         d_wout = g_out * scale
         dwout_ref[...] = d_wout
-        over_a(copy_s3, "recv")
-        sm32[...] = s3[...].reshape(SMALL, CH) * factor
-        dk = sm32[0:TAPS]
-        d_bin = jnp.concatenate([sm32[49 + q : 50 + q] for q in range(4)], 1)
-        d_gain, d_bias, d_cb, s_cot = (sm32[53 + q : 54 + q] for q in range(4))
-        d_bout = s_cot * scale
         d_ls = jnp.sum(g_out * wout_ref[...].astype(f32), 0, keepdims=True) + bout_ref[...] * s_cot
-        dk_ref[...] = dk
-        dbin_ref[...] = d_bin
-        dgain_ref[...] = d_gain
-        dbias_ref[...] = d_bias
-        dcb_ref[...] = d_cb
-        dbout_ref[...] = d_bout
         dls_ref[...] = d_ls
         squares = jnp.sum(d_win * d_win, 0, keepdims=True) + d_bin * d_bin
         squares = sum(squares[:, q * CH : (q + 1) * CH] for q in range(4))
@@ -455,7 +443,6 @@
         over_b(copy_w3, "done")
         over_a(copy_s1, "done")
         over_b(copy_s2, "done")
-        over_a(copy_s3, "done")
         for t in range(TC):
             store(t).wait()
 
@@ -496,10 +483,8 @@
             pltpu.VMEM((nb, wrows, HID), bf16),
             pltpu.VMEM((na, wrows, HID), bf16),
             pltpu.VMEM((nb, wrows, HID), bf16),
-            pltpu.VMEM((na, srows, CH), f32),
-            pltpu.VMEM((na, srows, CH), f32),
-            pltpu.VMEM((nb, srows, CH), f32),
-            pltpu.VMEM((na, srows, CH), f32),
+            pltpu.VMEM((na, SMALL, CH), bf16),
+            pltpu.VMEM((nb, SMALL, CH), bf16),
             dma((3, TC)),
             dma((6,)),
             dma((TC,)),
@@ -508,7 +493,7 @@
             dma((2,)),
             dma((2,)),
         ]
-        + [dma((n,)) for n in (nb, nb, na, na, nb, nb, na, na, nb, nb, na, na)],
+        + [dma((n,)) for n in (nb, nb, na, na, nb, nb, na, na, nb, nb)],
         compiler_params=pltpu.CompilerParams(
             collective_id=0, has_side_effects=True, vmem_limit_bytes=60 * 2**20
         ),
@@ -538,28 +523,39 @@
 
 def hand_on(*refs):
     n = len(RESULTS)
-    src, dst, sem = refs[:n], refs[n : 2 * n], refs[2 * n]
+    src, dst, stage, sem_in, sem_out = refs[:n], refs[n : 2 * n], refs[2 * n : 3 * n], refs[3 * n], refs[3 * n + 1]
     rows = LAT_ROWS // BANDS
-    copies = [
-        pltpu.make_async_copy(src[0].at[pl.ds(i * rows, rows)], dst[0].at[pl.ds(i * rows, rows)], sem.at[n + i])
-        for i in range(BANDS)
-    ]
-    copies += [pltpu.make_async_copy(src[i], dst[i], sem.at[i]) for i in range(1, n)]
-    for copy in copies:
-        copy.start()
-    for copy in copies:
-        copy.wait()
+
+    def parts(i):
+        return [pl.ds(j * rows, rows) for j in range(BANDS)] if i == 0 else [slice(None)]
+
+    hops = []
+    for i in range(n):
+        for j, part in enumerate(parts(i)):
+            slot = n + j if i == 0 else i
+            hops.append((
+                pltpu.make_async_copy(src[i].at[part], stage[i].at[part], sem_in.at[slot]),
+                pltpu.make_async_copy(stage[i].at[part], dst[i].at[part], sem_out.at[slot]),
+            ))
+    for first, _ in hops:
+        first.start()
+    for first, second in hops:
+        first.wait()
+        second.start()
+    for _, second in hops:
+        second.wait()
 
 
 def make_hand_on():
     n = len(RESULTS)
-    hbm = pl.BlockSpec(memory_space=pl.ANY)
+    hbm = pl.BlockSpec(memory_space=pltpu.HBM)
+    dma = pltpu.SemaphoreType.DMA((n + BANDS,))
     return pl.pallas_call(
         hand_on,
         in_specs=[hbm] * n,
         out_specs=[hbm] * n,
         out_shape=RESULTS,
-        scratch_shapes=[pltpu.SemaphoreType.DMA((n + BANDS,))],
+        scratch_shapes=[pltpu.VMEM(r.shape, r.dtype) for r in RESULTS] + [dma, dma],
         name="hand_on",
     )
 

time: 106 us -> 47.9 us (0.45)
  Pallas kernels: 105 us -> 46.9 us
    pallas_call x1, Pallas kernels: 60.4 us -> 3.32 us  [on_device(): finish(*outs)]
where the time goes in v3:
time: 47.9 us; the launch traced here: 47.6 us
  Pallas kernels  46.9 us (98%)
  between operations  0.66 us (1%)
    pallas_call x1, Pallas kernels, on_device(): call(conv_out, cotangent, field_in, kernel, line(ln_gain), line(ln_bias),...  43.6 us
    pallas_call x1, Pallas kernels, on_device(): finish(*outs)  3.32 us

profile of v3, /device:TPU:1, one launch (start us, length us, event | category | flops | bytes accessed | tf_op | source)
XLA Modules:
  0.0 47.6 jit_solution(11608818348809820369)
XLA Ops:
  0.6 43.6 %block_backward.1 = (bf16[96,56,128]{2,1,0:T(8,128)(2,1)}, f32[49,128]{1,0:T(8,128)}, f32[1,128]{1,0:T(1,128)}, f32[1,128]{1,0:T(1,128)}, f32[1,128]{1,0:T(1,128...) custom-call(bf16[96,56,128]{2,1,0:T(8,128)(2,1)} %x_hbm.1, ...), custom_call_target="tpu_custom_call" | custom-call | flops 6000000000 | bytes 6000000 | tf_op jit(solution)/shard_map/block_backward/pallas_call | solution.py:576
  44.2 3.3 %hand_on.1 = (bf16[96,56,128]{2,1,0:T(8,128)(2,1)}, f32[49,128]{1,0:T(8,128)}, f32[1,128]{1,0:T(1,128)}, f32[1,128]{1,0:T(1,128)}, f32[1,128]{1,0:T(1,128)}, /*i...) custom-call(bf16[96,56,128]{2,1,0:T(8,128)(2,1)} %get-tuple-element., ...), custom_call_target="tpu_custom_call" | custom-call | tf_op jit(solution)/shard_map/hand_on/pallas_call | solution.py:580

commit v4 on v3

--- a/solution.py
+++ b/solution.py
@@ -97,12 +97,14 @@
     factor = float(total_cells) ** (-0.5)
 
     def kernel(
-        x_hbm, c_hbm, f_hbm, ker_hbm, gain_ref, bias_ref, win_ref, bin_ref, wout_ref, bout_ref, ls_ref,
+        x_hbm, c_hbm, f_hbm, ker_hbm, gain_hbm, bias_hbm, win_hbm, bin_hbm, wout_hbm, bout_hbm, ls_hbm,
         cos_ref, mf_hbm, mg_hbm, mi_hbm, mk_hbm, md_hbm,
-        out_hbm, dk_ref, dcb_ref, dgain_ref, dbias_ref, dwin_ref, dbin_ref, dwout_ref, dbout_ref, dls_ref, norm_ref,
+        out_hbm, dk_hbm, dcb_hbm, dgain_hbm, dbias_hbm, dwin_hbm, dbin_hbm, dwout_hbm, dbout_hbm, dls_hbm, norm_hbm,
+        dk_ref, dcb_ref, dgain_ref, dbias_ref, dwin_ref, dbin_ref, dwout_ref, dbout_ref, dls_ref, norm_ref,
+        gain_ref, bias_ref, win_ref, bin_ref, wout_ref, bout_ref, ls_ref, dps, norms, rstds,
         xv, cv, fv, outv, dup, yb, mf, mg, mi, mk, md, ker, kpad, kh, acc, gw, gbin, small, sm32,
         hs, hr, vs, vr, ws, wr, w2, wf, s1, s2,
-        in_sem, const_sem, out_sem, h_send, h_recv, v_send, v_recv,
+        in_sem, const_sem, res_sem, out_sem, h_send, h_recv, v_send, v_recv,
         w1_send, w1_recv, w2_send, w2_recv, w3_send, w3_recv, s1_send, s1_recv, s2_send, s2_recv,
     ):
         lon, lat = lax.axis_index("lon"), lax.axis_index("lat")
@@ -125,15 +127,31 @@
             src, dst = ((x_hbm, xv), (c_hbm, cv), (f_hbm, fv))[which]
             return pltpu.make_async_copy(src.at[:, pl.ds(8 * t, 8), :], dst.at[t], in_sem.at[which, t])
 
-        consts = ((mf_hbm, mf), (mg_hbm, mg), (mk_hbm, mk), (ker_hbm, ker), (md_hbm, md), (mi_hbm, mi))
+        consts = (
+            (gain_hbm, gain_ref), (bias_hbm, bias_ref), (win_hbm, win_ref), (bin_hbm, bin_ref), (wout_hbm, wout_ref),
+            (ls_hbm, ls_ref), (bout_hbm, bout_ref),
+            (mf_hbm, mf), (mg_hbm, mg), (mk_hbm, mk), (ker_hbm, ker), (md_hbm, md), (mi_hbm, mi),
+        )
+        results = (
+            (dk_ref, dk_hbm), (dcb_ref, dcb_hbm), (dgain_ref, dgain_hbm), (dbias_ref, dbias_hbm), (dbin_ref, dbin_hbm),
+            (dbout_ref, dbout_hbm), (dwin_ref, dwin_hbm), (dwout_ref, dwout_hbm), (dls_ref, dls_hbm), (norm_ref, norm_hbm),
+        )
+
+        def give(i):
+            return pltpu.make_async_copy(*results[i], res_sem.at[i])
 
         def load_const(i):
             return pltpu.make_async_copy(*consts[i], const_sem.at[i])
 
-        for t in (0, TC - 1, *range(1, TC - 1)):
+        for t in (0, TC - 1):
             load(0, t).start()
             load(1, t).start()
-        for i in range(len(consts)):
+        for i in range(7):
+            load_const(i).start()
+        for t in range(1, TC - 1):
+            load(0, t).start()
+            load(1, t).start()
+        for i in range(7, len(consts)):
             load_const(i).start()
         for t in range(TC):
             load(2, t).start()
@@ -158,45 +176,52 @@
         mean_two = jnp.concatenate(
             [jnp.concatenate([third, none], 1), jnp.concatenate([none, third], 1)], 0
         )
-        gain, bias, scale = gain_ref[...], bias_ref[...], ls_ref[...]
         gw[...] = jnp.zeros_like(gw)
         gbin[...] = jnp.zeros_like(gbin)
         small[...] = jnp.zeros_like(small)
         acc[...] = jnp.zeros_like(acc)
         kpad[...] = jnp.zeros_like(kpad)
 
-        def mlp(parts):
-            def cells_of(ref):
-                return jnp.concatenate(
-                    [ref[t, pl.ds(r0, n)].astype(f32).reshape(n * 8, CH) for t, r0, n in parts], 0
-                )
-
-            value = cells_of(xv)
+        for i in range(7):
+            load_const(i).wait()
+        gain, bias, scale = gain_ref[...], bias_ref[...], ls_ref[...]
+        win_half, bin_half = win_ref[...] * jnp.asarray(0.5, bf16), bin_ref[...] * 0.5
+        wout_half = wout_ref[...] * jnp.asarray(0.5, bf16)
+
+        def cells_of(ref, parts):
+            return jnp.concatenate([ref[t, pl.ds(r0, n)].astype(f32).reshape(n * 8, CH) for t, r0, n in parts], 0)
+
+        def mlp_grads(parts):
+            value = cells_of(xv, parts)
             center = value - dot(value.astype(bf16), third)
             rstd = lax.rsqrt(dot((center * center).astype(bf16), third) + EPS)
             normed = center * rstd
             zed = (normed * gain + bias).astype(bf16)
-            cot = cells_of(cv)
+            cot = cells_of(cv, parts)
             cb = cot.astype(bf16)
             d_out = (cot * scale).astype(bf16)
             acts, dpres = [], []
             g_bin = jnp.zeros((8, HID), f32)
             sub = value.shape[0] // 2
             for s in range(0, value.shape[0], sub):
-                h = dot(zed[s : s + sub], win_ref[...]) + bin_ref[...]
-                d_act = dot_last(d_out[s : s + sub], wout_ref[...])
+                h = dot(zed[s : s + sub], win_half) + bin_half
+                d_act = dot_last(d_out[s : s + sub], wout_half)
                 h2 = h * h
-                inner = h * (ROOT + (ROOT * COEF) * h2)
-                wide = h * (2 * ROOT + (6 * ROOT * COEF) * h2)
-                gate = 0.5 * jnp.tanh(inner) + 0.5
-                d_pre = d_act * (gate * (1.0 + (1.0 - gate) * wide))
+                tangent = jnp.tanh(h * (2 * ROOT + (8 * ROOT * COEF) * h2))
+                wide = h * (2 * ROOT + (24 * ROOT * COEF) * h2)
+                above = 1.0 + tangent
+                d_pre = d_act * (above * (1.0 + (1.0 - tangent) * wide))
                 g_bin = g_bin + rows8(d_pre)
-                acts.append((h * gate).astype(bf16))
+                acts.append((h * above).astype(bf16))
                 dpres.append(d_pre.astype(bf16))
             act, d_pre = jnp.concatenate(acts, 0), jnp.concatenate(dpres, 0)
             gbin[...] += g_bin
             gw[CH:, :] += dot_rows(cb, act)
             gw[:CH, :] += dot_rows(zed, d_pre)
+            small[3] += rows8(cot)
+            return d_pre, normed, rstd
+
+        def mlp_du(parts, d_pre, normed, rstd):
             d_zed = dot_last(d_pre, win_ref[...])
             d_gain = d_zed * normed
             d_norm = d_zed * gain
@@ -211,12 +236,11 @@
             small[0] += rows8(d_gain)
             small[1] += rows8(d_zed)
             small[2] += rows8(du)
-            small[3] += rows8(cot)
 
         for t in (0, TC - 1):
             load(0, t).wait()
             load(1, t).wait()
-        mlp(RIM)
+        mlp_du(RIM, *mlp_grads(RIM))
 
         half = LAT_ROWS // 2
         low = lax.broadcasted_iota(jnp.int32, (half, 8, CH), 1) < 4
@@ -245,11 +269,18 @@
             load(0, t).wait()
             load(1, t).wait()
 
-        def mlp_middle(i, carry):
-            mlp([(t, i * half, half) for t in range(1, TC - 1)])
+        def middle_parts(i):
+            return [(t, i * half, half) for t in range(1, TC - 1)]
+
+        def middle_grads(i, carry):
+            dps[i], norms[i], rstds[i] = mlp_grads(middle_parts(i))
             return carry
 
-        lax.fori_loop(0, 2, mlp_middle, 0)
+        def middle_du(i, carry):
+            mlp_du(middle_parts(i), dps[i], norms[i], rstds[i])
+            return carry
+
+        lax.fori_loop(0, 2, middle_grads, 0)
 
         def copy_w1(b_to, b_from):
             return pltpu.make_async_remote_copy(
@@ -269,16 +300,16 @@
                 device_id=b_peer(b_to), device_id_type=MESH,
             )
 
-        def copy_s1(a_to, a_from):
+        def copy_s1(b_to, b_from):
             return pltpu.make_async_remote_copy(
-                src_ref=s1.at[a_me], dst_ref=s1.at[a_from], send_sem=s1_send.at[a_to], recv_sem=s1_recv.at[a_from],
+                src_ref=s1.at[b_me], dst_ref=s1.at[b_from], send_sem=s1_send.at[b_to], recv_sem=s1_recv.at[b_from],
+                device_id=b_peer(b_to), device_id_type=MESH,
+            )
+
+        def copy_s2(a_to, a_from):
+            return pltpu.make_async_remote_copy(
+                src_ref=s2.at[a_me], dst_ref=s2.at[a_from], send_sem=s2_send.at[a_to], recv_sem=s2_recv.at[a_from],
                 device_id=a_peer(a_to), device_id_type=MESH,
-            )
-
-        def copy_s2(b_to, b_from):
-            return pltpu.make_async_remote_copy(
-                src_ref=s2.at[b_me], dst_ref=s2.at[b_from], send_sem=s2_send.at[b_to], recv_sem=s2_recv.at[b_from],
-                device_id=b_peer(b_to), device_id_type=MESH,
             )
 
         def over(copy, act, me, size):
@@ -302,6 +333,7 @@
 
         ws[...] = gw[...].astype(bf16).reshape(nb, wrows, HID)
         over_b(copy_w1, "send")
+        lax.fori_loop(0, 2, middle_du, 0)
 
         copy_h(0).wait_recv()
         copy_h(1).wait_recv()
@@ -320,7 +352,7 @@
         copy_v(0).start()
         copy_v(1).start()
 
-        for i in range(len(consts)):
+        for i in range(7, len(consts)):
             load_const(i).wait()
         for t in range(TC):
             load(2, t).wait()
@@ -362,6 +394,11 @@
         lax.fori_loop(0, pairs - 1, middle, 0)
         lax.fori_loop(0, pairs - 1, sides, 0)
 
+        wr[b_me] = ws[b_me]
+        over_b(copy_w1, "recv")
+        w2[a_me] = jnp.sum(wr[...].astype(f32), 0).astype(bf16)
+        over_a(copy_w2, "send")
+
         copy_v(0).wait_recv()
         copy_v(1).wait_recv()
         zero = jnp.zeros((3, 64, CH), f32)
@@ -376,8 +413,8 @@
         for q in range(4):
             sm32[49 + q : 50 + q] = total[:, q * CH : (q + 1) * CH]
             sm32[53 + q : 54 + q] = jnp.sum(small[q], 0, keepdims=True)
-        s1[a_me] = sm32[...].astype(bf16)
-        over_a(copy_s1, "send")
+        s1[b_me] = sm32[...].astype(bf16)
+        over_b(copy_s1, "send")
 
         def store(t):
             return pltpu.make_async_copy(outv.at[t], out_hbm.at[:, pl.ds(8 * t, 8), :], out_sem.at[t])
@@ -394,46 +431,50 @@
             store(t).start()
             return carry
 
-        lax.fori_loop(0, 3, finish, 0)
-        wr[b_me] = ws[b_me]
-        over_b(copy_w1, "recv")
-        w2[a_me] = jnp.sum(wr[...].astype(f32), 0).astype(bf16)
-        over_a(copy_w2, "send")
-        lax.fori_loop(3, TC, finish, 0)
-        over_a(copy_s1, "recv")
-        s2[b_me] = jnp.sum(s1[...].astype(f32), 0).astype(bf16)
-        over_b(copy_s2, "send")
+        lax.fori_loop(0, TC, finish, 0)
         over_a(copy_w2, "recv")
         wf[b_me] = jnp.sum(w2[...].astype(f32), 0).astype(bf16)
         over_b(copy_w3, "send")
-
-        over_b(copy_s2, "recv")
+        over_b(copy_s1, "recv")
+        s2[a_me] = jnp.sum(s1[...].astype(f32), 0).astype(bf16)
+        over_a(copy_s2, "send")
+
+        over_b(copy_w3, "recv")
+        d_win = jnp.concatenate([wf[b].astype(f32) for b in range(nb // 2)], 0) * factor
+        dwin_ref[...] = d_win
+        give(6).start()
+        g_out = jnp.concatenate([wf[b].astype(f32) for b in range(nb // 2, nb)], 0) * factor
+        g_out = g_out.T
+        d_wout = g_out * scale
+        dwout_ref[...] = d_wout
+        give(7).start()
+        squares = jnp.sum(d_win * d_win, 0, keepdims=True)
+        squares = sum(squares[:, q * CH : (q + 1) * CH] for q in range(4))
+        squares = squares + jnp.sum(d_wout * d_wout, 0, keepdims=True)
+        g_ls = jnp.sum(g_out * wout_ref[...].astype(f32), 0, keepdims=True)
+        over_a(copy_s2, "recv")
         sm32[...] = jnp.sum(s2[...].astype(f32), 0) * factor
         dk = sm32[0:TAPS]
         d_bin = jnp.concatenate([sm32[49 + q : 50 + q] for q in range(4)], 1)
         d_gain, d_bias, d_cb, s_cot = (sm32[53 + q : 54 + q] for q in range(4))
         d_bout = s_cot * scale
+        d_ls = g_ls + bout_ref[...] * s_cot
         dk_ref[...] = dk
-        dbin_ref[...] = d_bin
+        dcb_ref[...] = d_cb
         dgain_ref[...] = d_gain
         dbias_ref[...] = d_bias
-        dcb_ref[...] = d_cb
+        dbin_ref[...] = d_bin
         dbout_ref[...] = d_bout
-        over_b(copy_w3, "recv")
-        d_win = jnp.concatenate([wf[b].astype(f32) for b in range(nb // 2)], 0) * factor
-        dwin_ref[...] = d_win
-        g_out = jnp.concatenate([wf[b].astype(f32) for b in range(nb // 2, nb)], 0) * factor
-        g_out = g_out.T
-        d_wout = g_out * scale
-        dwout_ref[...] = d_wout
-        d_ls = jnp.sum(g_out * wout_ref[...].astype(f32), 0, keepdims=True) + bout_ref[...] * s_cot
         dls_ref[...] = d_ls
-        squares = jnp.sum(d_win * d_win, 0, keepdims=True) + d_bin * d_bin
-        squares = sum(squares[:, q * CH : (q + 1) * CH] for q in range(4))
-        squares = squares + jnp.sum(d_wout * d_wout, 0, keepdims=True) + jnp.sum(dk * dk, 0, keepdims=True)
+        for i in (0, 1, 2, 3, 4, 5, 8):
+            give(i).start()
+        squares = squares + jnp.sum(dk * dk, 0, keepdims=True)
+        for q in range(4):
+            squares = squares + d_bin[:, q * CH : (q + 1) * CH] * d_bin[:, q * CH : (q + 1) * CH]
         for part in (d_gain, d_bias, d_cb, d_bout, d_ls):
             squares = squares + part * part
         norm_ref[...] = jnp.sqrt(jnp.sum(squares, 1, keepdims=True))
+        give(9).start()
 
         for side in range(2):
             copy_h(side).wait_send()
@@ -441,21 +482,34 @@
         over_b(copy_w1, "done")
         over_a(copy_w2, "done")
         over_b(copy_w3, "done")
-        over_a(copy_s1, "done")
-        over_b(copy_s2, "done")
+        over_b(copy_s1, "done")
+        over_a(copy_s2, "done")
         for t in range(TC):
             store(t).wait()
-
-    hbm, vmem, smem = (pl.BlockSpec(memory_space=m) for m in (pl.ANY, pltpu.VMEM, pltpu.SMEM))
+        for i in range(len(results)):
+            give(i).wait()
+
+    hbm, smem = pl.BlockSpec(memory_space=pl.ANY), pl.BlockSpec(memory_space=pltpu.SMEM)
     shape = jax.ShapeDtypeStruct
     dma = pltpu.SemaphoreType.DMA
     by_tile = (TC, LAT_ROWS, 8, CH)
     return pl.pallas_call(
         kernel,
-        in_specs=[hbm] * 4 + [vmem] * 7 + [smem] + [hbm] * 5,
-        out_specs=[hbm] + [vmem] * 10,
+        in_specs=[hbm] * 11 + [smem] + [hbm] * 5,
+        out_specs=[hbm] * 11,
         out_shape=RESULTS,
-        scratch_shapes=[
+        scratch_shapes=[pltpu.VMEM(r.shape, r.dtype) for r in RESULTS[1:]]
+        + [
+            pltpu.VMEM((1, CH), f32),
+            pltpu.VMEM((1, CH), f32),
+            pltpu.VMEM((CH, HID), bf16),
+            pltpu.VMEM((1, HID), f32),
+            pltpu.VMEM((HID, CH), bf16),
+            pltpu.VMEM((1, CH), f32),
+            pltpu.VMEM((1, CH), f32),
+            pltpu.VMEM((2, LAT_ROWS // 2 * (COLS - 16), HID), bf16),
+            pltpu.VMEM((2, LAT_ROWS // 2 * (COLS - 16), CH), f32),
+            pltpu.VMEM((2, LAT_ROWS // 2 * (COLS - 16), CH), f32),
             pltpu.VMEM(by_tile, bf16),
             pltpu.VMEM(by_tile, bf16),
             pltpu.VMEM(by_tile, bf16),
@@ -483,17 +537,18 @@
             pltpu.VMEM((nb, wrows, HID), bf16),
             pltpu.VMEM((na, wrows, HID), bf16),
             pltpu.VMEM((nb, wrows, HID), bf16),
+            pltpu.VMEM((nb, SMALL, CH), bf16),
             pltpu.VMEM((na, SMALL, CH), bf16),
-            pltpu.VMEM((nb, SMALL, CH), bf16),
             dma((3, TC)),
-            dma((6,)),
+            dma((13,)),
+            dma((len(RESULTS) - 1,)),
             dma((TC,)),
             dma((2,)),
             dma((2,)),
             dma((2,)),
             dma((2,)),
         ]
-        + [dma((n,)) for n in (nb, nb, na, na, nb, nb, na, na, nb, nb)],
+        + [dma((n,)) for n in (nb, nb, na, na, nb, nb, nb, nb, na, na)],
         compiler_params=pltpu.CompilerParams(
             collective_id=0, has_side_effects=True, vmem_limit_bytes=60 * 2**20
         ),

time: 47.9 us -> 44.7 us (0.933)
  Pallas kernels: 46.9 us -> 43.9 us
    pallas_call x1, Pallas kernels: 43.6 us -> 40.6 us  [on_device(): call(conv_out, cotangent, field_in, kernel, line(ln_gain), line(ln_bias),...]
where the time goes in v4:
time: 44.7 us; the launch traced here: 44.6 us
  Pallas kernels  43.9 us (98%)
  between operations  0.66 us (1%)
    pallas_call x1, Pallas kernels, on_device(): call(conv_out, cotangent, field_in, kernel, line(ln_gain), line(ln_bias),...  40.6 us
    pallas_call x1, Pallas kernels, on_device(): finish(*outs)  3.32 us

profile of v4, /device:TPU:1, one launch (start us, length us, event | category | flops | bytes accessed | tf_op | source)
XLA Modules:
  0.0 44.6 jit_solution(14223552440385742247)
XLA Ops:
  0.6 40.6 %block_backward.1 = (bf16[96,56,128]{2,1,0:T(8,128)(2,1)}, f32[49,128]{1,0:T(8,128)}, f32[1,128]{1,0:T(1,128)}, f32[1,128]{1,0:T(1,128)}, f32[1,128]{1,0:T(1,128...) custom-call(bf16[96,56,128]{2,1,0:T(8,128)(2,1)} %x_hbm.1, ...), custom_call_target="tpu_custom_call" | custom-call | flops 6000000000 | bytes 6000000 | tf_op jit(solution)/shard_map/block_backward/pallas_call | solution.py:631
  41.2 3.3 %hand_on.1 = (bf16[96,56,128]{2,1,0:T(8,128)(2,1)}, f32[49,128]{1,0:T(8,128)}, f32[1,128]{1,0:T(1,128)}, f32[1,128]{1,0:T(1,128)}, f32[1,128]{1,0:T(1,128)}, /*i...) custom-call(bf16[96,56,128]{2,1,0:T(8,128)(2,1)} %get-tuple-element., ...), custom_call_target="tpu_custom_call" | custom-call | tf_op jit(solution)/shard_map/hand_on/pallas_call | solution.py:635

commit v5 on v4

--- a/solution.py
+++ b/solution.py
@@ -60,13 +60,14 @@
     taps = interleave(np.cos(a), -np.sin(a) * twin)
     taps_inv = interleave(np.cos(a) * weight, -np.sin(a) * weight * twin).T
     area = N * N
-    return (
-        (fwd * SCALE).astype(ml_dtypes.bfloat16),
-        (fwd_tile * SCALE).astype(ml_dtypes.bfloat16),
-        (inv * area * SCALE).astype(ml_dtypes.bfloat16),
-        (np.pad(taps, ((0, 0), (0, 7))) / (area * SCALE * SCALE)).astype(np.float32),
-        (np.pad(taps_inv, ((0, 7), (0, 0))) / (SCALE * SCALE)).astype(np.float32),
-    )
+    low = np.zeros((FREQ + OUT * OUT, 384))
+    low[:FREQ, : N * 16] = fwd * SCALE
+    low[:FREQ, 256 : 256 + OUT * OUT] = fwd_tile * SCALE
+    low[FREQ:, :FREQ] = inv * area * SCALE
+    high = np.zeros((FREQ + 56, FREQ))
+    high[:FREQ, :TAPS] = taps / (area * SCALE * SCALE)
+    high[FREQ : FREQ + TAPS] = taps_inv / (SCALE * SCALE)
+    return low.astype(ml_dtypes.bfloat16), high.astype(np.float32)
 
 
 def dot(a, b):
@@ -98,11 +99,11 @@
 
     def kernel(
         x_hbm, c_hbm, f_hbm, ker_hbm, gain_hbm, bias_hbm, win_hbm, bin_hbm, wout_hbm, bout_hbm, ls_hbm,
-        cos_ref, mf_hbm, mg_hbm, mi_hbm, mk_hbm, md_hbm,
-        out_hbm, dk_hbm, dcb_hbm, dgain_hbm, dbias_hbm, dwin_hbm, dbin_hbm, dwout_hbm, dbout_hbm, dls_hbm, norm_hbm,
-        dk_ref, dcb_ref, dgain_ref, dbias_ref, dwin_ref, dbin_ref, dwout_ref, dbout_ref, dls_ref, norm_ref,
+        cos_ref, low_hbm, high_hbm,
+        out_hbm, dwin_hbm, dwout_hbm, rest_hbm,
+        dwin_ref, dwout_ref, rest_ref,
         gain_ref, bias_ref, win_ref, bin_ref, wout_ref, bout_ref, ls_ref, dps, norms, rstds,
-        xv, cv, fv, outv, dup, yb, mf, mg, mi, mk, md, ker, kpad, kh, acc, gw, gbin, small, sm32,
+        xv, cv, fv, outv, dup, yb, low_ref, high_ref, ker, kpad, kh, acc, gw, gbin, small, sm32,
         hs, hr, vs, vr, ws, wr, w2, wf, s1, s2,
         in_sem, const_sem, res_sem, out_sem, h_send, h_recv, v_send, v_recv,
         w1_send, w1_recv, w2_send, w2_recv, w3_send, w3_recv, s1_send, s1_recv, s2_send, s2_recv,
@@ -123,19 +124,20 @@
         right, left = lax.rem(lon + 1, nlon), lax.rem(lon + nlon - 1, nlon)
         down, up = lax.rem(lat + 1, nlat), lax.rem(lat + nlat - 1, nlat)
 
-        def load(which, t):
-            src, dst = ((x_hbm, xv), (c_hbm, cv), (f_hbm, fv))[which]
-            return pltpu.make_async_copy(src.at[:, pl.ds(8 * t, 8), :], dst.at[t], in_sem.at[which, t])
+        sides_x, middle_x = (pl.ds(0, 8), pl.ds(COLS - 8, 8)), pl.ds(8, COLS - 16)
+        loads = [(x_hbm, xv, sides_x[0]), (c_hbm, cv, sides_x[0]), (x_hbm, xv, sides_x[1]), (c_hbm, cv, sides_x[1])]
+        loads += [(x_hbm, xv, middle_x), (c_hbm, cv, middle_x), (f_hbm, fv, pl.ds(0, COLS))]
+
+        def load(i):
+            src, dst, cols = loads[i]
+            return pltpu.make_async_copy(src.at[:, cols, :], dst.at[:, cols, :], in_sem.at[i])
 
         consts = (
             (gain_hbm, gain_ref), (bias_hbm, bias_ref), (win_hbm, win_ref), (bin_hbm, bin_ref), (wout_hbm, wout_ref),
             (ls_hbm, ls_ref), (bout_hbm, bout_ref),
-            (mf_hbm, mf), (mg_hbm, mg), (mk_hbm, mk), (ker_hbm, ker), (md_hbm, md), (mi_hbm, mi),
+            (low_hbm, low_ref), (high_hbm, high_ref), (ker_hbm, ker),
         )
-        results = (
-            (dk_ref, dk_hbm), (dcb_ref, dcb_hbm), (dgain_ref, dgain_hbm), (dbias_ref, dbias_hbm), (dbin_ref, dbin_hbm),
-            (dbout_ref, dbout_hbm), (dwin_ref, dwin_hbm), (dwout_ref, dwout_hbm), (dls_ref, dls_hbm), (norm_ref, norm_hbm),
-        )
+        results = ((dwin_ref, dwin_hbm), (dwout_ref, dwout_hbm), (rest_ref, rest_hbm))
 
         def give(i):
             return pltpu.make_async_copy(*results[i], res_sem.at[i])
@@ -143,18 +145,14 @@
         def load_const(i):
             return pltpu.make_async_copy(*consts[i], const_sem.at[i])
 
-        for t in (0, TC - 1):
-            load(0, t).start()
-            load(1, t).start()
+        for i in range(4):
+            load(i).start()
         for i in range(7):
             load_const(i).start()
-        for t in range(1, TC - 1):
-            load(0, t).start()
-            load(1, t).start()
+        for i in range(4, len(loads)):
+            load(i).start()
         for i in range(7, len(consts)):
             load_const(i).start()
-        for t in range(TC):
-            load(2, t).start()
 
         barrier = pltpu.get_barrier_semaphore()
         for peer in ((right, lat), (left, lat), (lon, down), (lon, up)):
@@ -189,7 +187,7 @@
         wout_half = wout_ref[...] * jnp.asarray(0.5, bf16)
 
         def cells_of(ref, parts):
-            return jnp.concatenate([ref[t, pl.ds(r0, n)].astype(f32).reshape(n * 8, CH) for t, r0, n in parts], 0)
+            return jnp.concatenate([ref[pl.ds(r0, n), 8 * t : 8 * t + 8, :].astype(f32).reshape(n * 8, CH) for t, r0, n in parts], 0)
 
         def mlp_grads(parts):
             value = cells_of(xv, parts)
@@ -237,9 +235,8 @@
             small[1] += rows8(d_zed)
             small[2] += rows8(du)
 
-        for t in (0, TC - 1):
-            load(0, t).wait()
-            load(1, t).wait()
+        for i in range(4):
+            load(i).wait()
         mlp_du(RIM, *mlp_grads(RIM))
 
         half = LAT_ROWS // 2
@@ -265,9 +262,8 @@
         hs[1] = jnp.where(low, pltpu.roll(second, 4, 1), first).reshape(half * 8, CH).astype(bf16)
         copy_h(1).start()
 
-        for t in range(1, TC - 1):
-            load(0, t).wait()
-            load(1, t).wait()
+        load(4).wait()
+        load(5).wait()
 
         def middle_parts(i):
             return [(t, i * half, half) for t in range(1, TC - 1)]
@@ -354,23 +350,22 @@
 
         for i in range(7, len(consts)):
             load_const(i).wait()
-        for t in range(TC):
-            load(2, t).wait()
+        load(6).wait()
         kpad[0:TAPS] = ker[...]
-        kh[...] = dot_exact(mk[...], kpad[...])
+        kh[...] = dot_exact(high_ref[0:FREQ, 0:56], kpad[...])
 
         def tile_pair(slot, i0, i1, t):
             def window(i):
                 return dup[pl.ds(i * OUT, N), 8 * t : 8 * t + 16, :].reshape(N * 16, CH).astype(bf16)
 
             def field(i):
-                tile = fv[t, pl.ds(i * OUT, OUT)].astype(f32)
+                tile = fv[pl.ds(i * OUT, OUT), 8 * t : 8 * t + 8, :].astype(f32)
                 tile = [tile[r] * cos_ref[lat * LAT_ROWS + i * OUT + r] for r in range(OUT)]
                 return jnp.concatenate(tile, 0).astype(bf16)
 
             shape = (PAIRS // 8, 2, 8, 2 * CH)
-            w = dot(mf[...], jnp.concatenate([window(i0), window(i1)], 1)).reshape(shape)
-            g = dot(mg[...], jnp.concatenate([field(i0), field(i1)], 1)).reshape(shape)
+            w = dot(low_ref[0:FREQ, 0 : N * 16], jnp.concatenate([window(i0), window(i1)], 1)).reshape(shape)
+            g = dot(low_ref[0:FREQ, 256 : 256 + OUT * OUT], jnp.concatenate([field(i0), field(i1)], 1)).reshape(shape)
             k = kh[...].reshape(PAIRS // 8, 2, 8, CH)
             k = jnp.concatenate([k, k], -1)
             w_re, w_im, g_re, g_im, k_re, k_im = w[:, 0], w[:, 1], g[:, 0], g[:, 1], k[:, 0], k[:, 1]
@@ -394,11 +389,6 @@
         lax.fori_loop(0, pairs - 1, middle, 0)
         lax.fori_loop(0, pairs - 1, sides, 0)
 
-        wr[b_me] = ws[b_me]
-        over_b(copy_w1, "recv")
-        w2[a_me] = jnp.sum(wr[...].astype(f32), 0).astype(bf16)
-        over_a(copy_w2, "send")
-
         copy_v(0).wait_recv()
         copy_v(1).wait_recv()
         zero = jnp.zeros((3, 64, CH), f32)
@@ -408,7 +398,7 @@
             tile_pair(t * pairs + pairs - 1, 0, TL - 1, t)
 
         sm32[...] = jnp.zeros_like(sm32)
-        sm32[0:56] = dot_exact(md[...], acc[...])
+        sm32[0:56] = dot_exact(high_ref[FREQ : FREQ + 56, :], acc[...])
         total = jnp.sum(gbin[...], 0, keepdims=True)
         for q in range(4):
             sm32[49 + q : 50 + q] = total[:, q * CH : (q + 1) * CH]
@@ -416,22 +406,31 @@
         s1[b_me] = sm32[...].astype(bf16)
         over_b(copy_s1, "send")
 
-        def store(t):
-            return pltpu.make_async_copy(outv.at[t], out_hbm.at[:, pl.ds(8 * t, 8), :], out_sem.at[t])
-
-        def finish(t, carry):
-            for j in range(pairs):
-                conv = dot(mi[...], yb[t * pairs + j]).reshape(OUT, OUT, 2 * CH)
-                ends = (0, TL - 1) if j == pairs - 1 else (1 + 2 * j, 2 + 2 * j)
+        wr[b_me] = ws[b_me]
+        over_b(copy_w1, "recv")
+        w2[a_me] = jnp.sum(wr[...].astype(f32), 0).astype(bf16)
+        over_a(copy_w2, "send")
+
+        def store(j):
+            n = OUT if j >= pairs - 1 else 2 * OUT
+            at = (0, LAT_ROWS - OUT)[j - pairs + 1] if j >= pairs - 1 else (1 + 2 * j) * OUT
+            return pltpu.make_async_copy(outv.at[pl.ds(at, n)], out_hbm.at[pl.ds(at, n)], out_sem.at[j])
+
+        def finish(j, ends):
+            for t in range(TC):
+                conv = dot(low_ref[FREQ:, 0:FREQ], yb[t * pairs + j]).reshape(OUT, OUT, 2 * CH)
                 for n, i in enumerate(ends):
-                    cot = cv[t, i * OUT : (i + 1) * OUT].astype(f32)
+                    cot = cv[i * OUT : (i + 1) * OUT, 8 * t : 8 * t + 8, :].astype(f32)
                     part = conv[:, :, n * CH : (n + 1) * CH]
                     value = [cot[r] + part[r] * cos_ref[lat * LAT_ROWS + i * OUT + r] for r in range(OUT)]
-                    outv[t, i * OUT : (i + 1) * OUT] = jnp.stack(value, 0).astype(bf16)
-            store(t).start()
-            return carry
-
-        lax.fori_loop(0, TC, finish, 0)
+                    outv[i * OUT : (i + 1) * OUT, 8 * t : 8 * t + 8, :] = jnp.stack(value, 0).astype(bf16)
+
+        for j in range(pairs - 1):
+            finish(j, (1 + 2 * j, 2 + 2 * j))
+            store(j).start()
+        finish(pairs - 1, (0, TL - 1))
+        store(pairs - 1).start()
+        store(pairs).start()
         over_a(copy_w2, "recv")
         wf[b_me] = jnp.sum(w2[...].astype(f32), 0).astype(bf16)
         over_b(copy_w3, "send")
@@ -442,12 +441,12 @@
         over_b(copy_w3, "recv")
         d_win = jnp.concatenate([wf[b].astype(f32) for b in range(nb // 2)], 0) * factor
         dwin_ref[...] = d_win
-        give(6).start()
+        give(0).start()
         g_out = jnp.concatenate([wf[b].astype(f32) for b in range(nb // 2, nb)], 0) * factor
         g_out = g_out.T
         d_wout = g_out * scale
         dwout_ref[...] = d_wout
-        give(7).start()
+        give(1).start()
         squares = jnp.sum(d_win * d_win, 0, keepdims=True)
         squares = sum(squares[:, q * CH : (q + 1) * CH] for q in range(4))
         squares = squares + jnp.sum(d_wout * d_wout, 0, keepdims=True)
@@ -459,22 +458,16 @@
         d_gain, d_bias, d_cb, s_cot = (sm32[53 + q : 54 + q] for q in range(4))
         d_bout = s_cot * scale
         d_ls = g_ls + bout_ref[...] * s_cot
-        dk_ref[...] = dk
-        dcb_ref[...] = d_cb
-        dgain_ref[...] = d_gain
-        dbias_ref[...] = d_bias
-        dbin_ref[...] = d_bin
-        dbout_ref[...] = d_bout
-        dls_ref[...] = d_ls
-        for i in (0, 1, 2, 3, 4, 5, 8):
-            give(i).start()
+        rest_ref[...] = sm32[...]
+        rest_ref[56:57] = d_bout
+        rest_ref[57:58] = d_ls
         squares = squares + jnp.sum(dk * dk, 0, keepdims=True)
         for q in range(4):
             squares = squares + d_bin[:, q * CH : (q + 1) * CH] * d_bin[:, q * CH : (q + 1) * CH]
         for part in (d_gain, d_bias, d_cb, d_bout, d_ls):
             squares = squares + part * part
-        norm_ref[...] = jnp.sqrt(jnp.sum(squares, 1, keepdims=True))
-        give(9).start()
+        rest_ref[58:59] = jnp.broadcast_to(jnp.sqrt(jnp.sum(squares, 1, keepdims=True)), (1, CH))
+        give(2).start()
 
         for side in range(2):
             copy_h(side).wait_send()
@@ -484,21 +477,21 @@
         over_b(copy_w3, "done")
         over_b(copy_s1, "done")
         over_a(copy_s2, "done")
-        for t in range(TC):
-            store(t).wait()
+        for j in range(pairs + 1):
+            store(j).wait()
         for i in range(len(results)):
             give(i).wait()
 
     hbm, smem = pl.BlockSpec(memory_space=pl.ANY), pl.BlockSpec(memory_space=pltpu.SMEM)
     shape = jax.ShapeDtypeStruct
     dma = pltpu.SemaphoreType.DMA
-    by_tile = (TC, LAT_ROWS, 8, CH)
+    field = (LAT_ROWS, COLS, CH)
     return pl.pallas_call(
         kernel,
-        in_specs=[hbm] * 11 + [smem] + [hbm] * 5,
-        out_specs=[hbm] * 11,
-        out_shape=RESULTS,
-        scratch_shapes=[pltpu.VMEM(r.shape, r.dtype) for r in RESULTS[1:]]
+        in_specs=[hbm] * 11 + [smem] + [hbm] * 2,
+        out_specs=[hbm] * 4,
+        out_shape=HANDED,
+        scratch_shapes=[pltpu.VMEM(r.shape, r.dtype) for r in HANDED[1:]]
         + [
             pltpu.VMEM((1, CH), f32),
             pltpu.VMEM((1, CH), f32),
@@ -510,17 +503,14 @@
             pltpu.VMEM((2, LAT_ROWS // 2 * (COLS - 16), HID), bf16),
             pltpu.VMEM((2, LAT_ROWS // 2 * (COLS - 16), CH), f32),
             pltpu.VMEM((2, LAT_ROWS // 2 * (COLS - 16), CH), f32),
-            pltpu.VMEM(by_tile, bf16),
-            pltpu.VMEM(by_tile, bf16),
-            pltpu.VMEM(by_tile, bf16),
-            pltpu.VMEM(by_tile, bf16),
+            pltpu.VMEM(field, bf16),
+            pltpu.VMEM(field, bf16),
+            pltpu.VMEM(field, bf16),
+            pltpu.VMEM(field, bf16),
             pltpu.VMEM((LAT_ROWS + 6, COLS + 8, CH), f32),
             pltpu.VMEM((TL * TC // 2, FREQ, 2 * CH), bf16),
-            pltpu.VMEM((FREQ, N * 16), bf16),
-            pltpu.VMEM((FREQ, OUT * OUT), bf16),
-            pltpu.VMEM((OUT * OUT, FREQ), bf16),
-            pltpu.VMEM((FREQ, 56), f32),
-            pltpu.VMEM((56, FREQ), f32),
+            pltpu.VMEM((FREQ + OUT * OUT, 384), bf16),
+            pltpu.VMEM((FREQ + 56, FREQ), f32),
             pltpu.VMEM((TAPS, CH), f32),
             pltpu.VMEM((56, CH), f32),
             pltpu.VMEM((FREQ, CH), f32),
@@ -539,9 +529,9 @@
             pltpu.VMEM((nb, wrows, HID), bf16),
             pltpu.VMEM((nb, SMALL, CH), bf16),
             pltpu.VMEM((na, SMALL, CH), bf16),
-            dma((3, TC)),
-            dma((13,)),
-            dma((len(RESULTS) - 1,)),
+            dma((7,)),
+            dma((10,)),
+            dma((3,)),
             dma((TC,)),
             dma((2,)),
             dma((2,)),
@@ -573,44 +563,61 @@
         ((1, 1), f32),
     )
 ]
-BANDS = 6
+HANDED = [RESULTS[0], RESULTS[5], RESULTS[7], jax.ShapeDtypeStruct((SMALL, CH), f32)]
+ROWS = ((2, 55), (3, 53), (4, 54), (8, 56), (9, 57))
+BANDS = 4
 
 
 def hand_on(*refs):
-    n = len(RESULTS)
-    src, dst, stage, sem_in, sem_out = refs[:n], refs[n : 2 * n], refs[2 * n : 3 * n], refs[3 * n], refs[3 * n + 1]
+    n, m = len(RESULTS), len(HANDED)
+    src, dst = refs[:m], refs[m : m + n]
+    stage, lines, sem_in, sem_out = refs[m + n : 2 * m + n], refs[2 * m + n : -2], refs[-2], refs[-1]
     rows = LAT_ROWS // BANDS
-
-    def parts(i):
-        return [pl.ds(j * rows, rows) for j in range(BANDS)] if i == 0 else [slice(None)]
-
     hops = []
-    for i in range(n):
-        for j, part in enumerate(parts(i)):
-            slot = n + j if i == 0 else i
+    for i, to in enumerate((0, 5, 7)):
+        for j in range(BANDS if i == 0 else 1):
+            part = pl.ds(j * rows, rows) if i == 0 else slice(None)
+            slot = n + j if i == 0 else to
             hops.append((
                 pltpu.make_async_copy(src[i].at[part], stage[i].at[part], sem_in.at[slot]),
-                pltpu.make_async_copy(stage[i].at[part], dst[i].at[part], sem_out.at[slot]),
+                pltpu.make_async_copy(stage[i].at[part], dst[to].at[part], sem_out.at[slot]),
             ))
+    block_in = pltpu.make_async_copy(src[3], stage[3], sem_in.at[0])
+    block_in.start()
     for first, _ in hops:
         first.start()
+    block_in.wait()
+    block = stage[3]
+    lines[0][...] = block[0:TAPS]
+    lines[1][...] = jnp.concatenate([block[49 + q : 50 + q] for q in range(4)], 1)
+    lines[2][...] = block[58:59, 0:1]
+    for line, (_, row) in zip(lines[3:], ROWS):
+        line[...] = block[row : row + 1]
+    outs = [second for _, second in hops]
+    small = [
+        pltpu.make_async_copy(line, dst[to], sem_out.at[to])
+        for line, to in zip(lines, (1, 6, 10) + tuple(to for to, _ in ROWS))
+    ]
+    for copy in small:
+        copy.start()
     for first, second in hops:
         first.wait()
         second.start()
-    for _, second in hops:
-        second.wait()
+    for copy in small + outs:
+        copy.wait()
 
 
 def make_hand_on():
     n = len(RESULTS)
     hbm = pl.BlockSpec(memory_space=pltpu.HBM)
     dma = pltpu.SemaphoreType.DMA((n + BANDS,))
+    order = (1, 6, 10) + tuple(to for to, _ in ROWS)
     return pl.pallas_call(
         hand_on,
-        in_specs=[hbm] * n,
+        in_specs=[hbm] * len(HANDED),
         out_specs=[hbm] * n,
         out_shape=RESULTS,
-        scratch_shapes=[pltpu.VMEM(r.shape, r.dtype) for r in RESULTS] + [dma, dma],
+        scratch_shapes=[pltpu.VMEM(r.shape, r.dtype) for r in HANDED + [RESULTS[i] for i in order]] + [dma, dma],
         name="hand_on",
     )
 
@@ -622,7 +629,7 @@
     total_rows, total_cols = LAT_ROWS * nlat, COLS * nlon
     call = make_kernel(nz, nx, nyh, nyl, ncore, total_rows * total_cols)
     finish = make_hand_on()
-    fwd, fwd_tile, inv, taps, taps_inv = tables()
+    low, high = tables()
     place = (np.arange(total_rows, dtype=np.float32) + np.float32(0.5)) / np.float32(total_rows) - np.float32(0.5)
     weight = np.cos(np.float32(math.pi) * place).astype(np.float32)
 
@@ -630,7 +637,7 @@
         line = lambda v: v.reshape(1, -1)
         outs = call(
             conv_out, cotangent, field_in, kernel, line(ln_gain), line(ln_bias), w_in, line(b_in),
-            w_out, line(b_out), line(layer_scale), weight, fwd, fwd_tile, inv, taps, taps_inv,
+            w_out, line(b_out), line(layer_scale), weight, low, high,
         )
         d_field, d_kernel, d_cb, d_gain, d_bias, d_win, d_bin, d_wout, d_bout, d_ls, norm = finish(*outs)
         wide = lambda v: v.reshape(-1)

time: 44.7 us -> 42.9 us (0.960)
  Pallas kernels: 43.9 us -> 42.1 us
    pallas_call x1, Pallas kernels: 40.6 us -> 39.6 us  [on_device(): call(conv_out, cotangent, field_in, kernel, line(ln_gain), line(ln_bias),...]
    pallas_call x1, Pallas kernels: 3.32 us -> 2.51 us  [on_device(): finish(*outs)]
where the time goes in v5:
time: 42.9 us; the launch traced here: 42.7 us
  Pallas kernels  42.1 us (98%)
  between operations  0.66 us (2%)
    pallas_call x1, Pallas kernels, on_device(): call(conv_out, cotangent, field_in, kernel, line(ln_gain), line(ln_bias),...  39.6 us
    pallas_call x1, Pallas kernels, on_device(): finish(*outs)  2.51 us

profile of v5, /device:TPU:1, one launch (start us, length us, event | category | flops | bytes accessed | tf_op | source)
XLA Modules:
  0.0 42.7 jit_solution(5920991820272578856)
XLA Ops:
  0.6 39.6 %block_backward.1 = (bf16[96,56,128]{2,1,0:T(8,128)(2,1)}, f32[128,512]{1,0:T(8,128)}, f32[512,128]{1,0:T(8,128)}, f32[64,128]{1,0:T(8,128)}) custom-call(bf16[96,56,128]{2,1,0:T(8,128)(2,1)} %x_hbm.1, bf16[96,56,128]{2,1,0:T(8,128)(2,1)} %c_hbm.1, bf16[96,56,128]{2,1,0:T(8,128)(2,1)} %f_hbm.1, f32[49,128]{1,0:T(8,128)} %ker_hbm.1, f32[1,128]{1,0:T(1,128)} %bitcast.14, ...), custom_call_target="tpu_custom_call" | custom-call | flops 6000000000 | bytes 6000000 | tf_op jit(solution)/shard_map/block_backward/pallas_call | solution.py:638
  40.2 2.5 %hand_on.1 = (bf16[96,56,128]{2,1,0:T(8,128)(2,1)}, f32[49,128]{1,0:T(8,128)}, f32[1,128]{1,0:T(1,128)}, f32[1,128]{1,0:T(1,128)}, f32[1,128]{1,0:T(1,128)}, /*i...) custom-call(bf16[96,56,128]{2,1,0:T(8,128)(2,1)} %get-tuple-element., ...), custom_call_target="tpu_custom_call" | custom-call | tf_op jit(solution)/shard_map/hand_on/pallas_call | solution.py:642

commit v6 on v5

--- a/solution.py
+++ b/solution.py
@@ -280,46 +280,52 @@
 
         def copy_w1(b_to, b_from):
             return pltpu.make_async_remote_copy(
-                src_ref=ws.at[b_to], dst_ref=wr.at[b_from], send_sem=w1_send.at[b_to], recv_sem=w1_recv.at[b_from],
+                src_ref=ws.at[b_to], dst_ref=wr.at[b_from], send_sem=w1_send.at[0], recv_sem=w1_recv.at[0],
                 device_id=b_peer(b_to), device_id_type=MESH,
             )
 
         def copy_w2(a_to, a_from):
             return pltpu.make_async_remote_copy(
-                src_ref=w2.at[a_me], dst_ref=w2.at[a_from], send_sem=w2_send.at[a_to], recv_sem=w2_recv.at[a_from],
+                src_ref=w2.at[a_me], dst_ref=w2.at[a_from], send_sem=w2_send.at[0], recv_sem=w2_recv.at[0],
                 device_id=a_peer(a_to), device_id_type=MESH,
             )
 
         def copy_w3(b_to, b_from):
             return pltpu.make_async_remote_copy(
-                src_ref=wf.at[b_me], dst_ref=wf.at[b_from], send_sem=w3_send.at[b_to], recv_sem=w3_recv.at[b_from],
+                src_ref=wf.at[b_me], dst_ref=wf.at[b_from], send_sem=w3_send.at[0], recv_sem=w3_recv.at[0],
                 device_id=b_peer(b_to), device_id_type=MESH,
             )
 
         def copy_s1(b_to, b_from):
             return pltpu.make_async_remote_copy(
-                src_ref=s1.at[b_me], dst_ref=s1.at[b_from], send_sem=s1_send.at[b_to], recv_sem=s1_recv.at[b_from],
+                src_ref=s1.at[b_me], dst_ref=s1.at[b_from], send_sem=s1_send.at[0], recv_sem=s1_recv.at[0],
                 device_id=b_peer(b_to), device_id_type=MESH,
             )
 
         def copy_s2(a_to, a_from):
             return pltpu.make_async_remote_copy(
-                src_ref=s2.at[a_me], dst_ref=s2.at[a_from], send_sem=s2_send.at[a_to], recv_sem=s2_recv.at[a_from],
+                src_ref=s2.at[a_me], dst_ref=s2.at[a_from], send_sem=s2_send.at[0], recv_sem=s2_recv.at[0],
                 device_id=a_peer(a_to), device_id_type=MESH,
             )
 
+        ends = {
+            copy_w1: (wr, w1_send, w1_recv), copy_w2: (w2, w2_send, w2_recv), copy_w3: (wf, w3_send, w3_recv),
+            copy_s1: (s1, s1_send, s1_recv), copy_s2: (s2, s2_send, s2_recv),
+        }
+
         def over(copy, act, me, size):
-            def body(d, carry):
-                peer = lax.rem(me + d, size)
-                if act == "send":
-                    copy(peer, me).start()
-                elif act == "recv":
-                    copy(peer, peer).wait_recv()
-                else:
-                    copy(peer, me).wait_send()
-                return carry
-
-            lax.fori_loop(1, size, body, 0)
+            if act == "send":
+
+                def body(d, carry):
+                    copy(lax.rem(me + d, size), me).start()
+                    return carry
+
+                lax.fori_loop(1, size, body, 0)
+            else:
+                buf, sent, received = ends[copy]
+                others = buf.at[pl.ds(0, size - 1)]
+                sem = received if act == "recv" else sent
+                pltpu.make_async_copy(others, others, sem.at[0]).wait()
 
         def over_a(copy, act):
             over(copy, act, a_me, na)
@@ -431,6 +437,12 @@
         finish(pairs - 1, (0, TL - 1))
         store(pairs - 1).start()
         store(pairs).start()
+        for side in range(2):
+            copy_h(side).wait_send()
+            copy_v(side).wait_send()
+        over_b(copy_w1, "done")
+        over_b(copy_s1, "done")
+        over_a(copy_w2, "done")
         over_a(copy_w2, "recv")
         wf[b_me] = jnp.sum(w2[...].astype(f32), 0).astype(bf16)
         over_b(copy_w3, "send")
@@ -438,6 +450,9 @@
         s2[a_me] = jnp.sum(s1[...].astype(f32), 0).astype(bf16)
         over_a(copy_s2, "send")
 
+        for j in range(pairs + 1):
+            store(j).wait()
+        over_b(copy_w3, "done")
         over_b(copy_w3, "recv")
         d_win = jnp.concatenate([wf[b].astype(f32) for b in range(nb // 2)], 0) * factor
         dwin_ref[...] = d_win
@@ -469,16 +484,7 @@
         rest_ref[58:59] = jnp.broadcast_to(jnp.sqrt(jnp.sum(squares, 1, keepdims=True)), (1, CH))
         give(2).start()
 
-        for side in range(2):
-            copy_h(side).wait_send()
-            copy_v(side).wait_send()
-        over_b(copy_w1, "done")
-        over_a(copy_w2, "done")
-        over_b(copy_w3, "done")
-        over_b(copy_s1, "done")
         over_a(copy_s2, "done")
-        for j in range(pairs + 1):
-            store(j).wait()
         for i in range(len(results)):
             give(i).wait()
 
@@ -538,7 +544,7 @@
             dma((2,)),
             dma((2,)),
         ]
-        + [dma((n,)) for n in (nb, nb, na, na, nb, nb, nb, nb, na, na)],
+        + [dma((1,)) for _ in range(10)],
         compiler_params=pltpu.CompilerParams(
             collective_id=0, has_side_effects=True, vmem_limit_bytes=60 * 2**20
         ),

time: 42.9 us -> 41.7 us (0.972)
  Pallas kernels: 42.1 us -> 40.8 us
    pallas_call x1, Pallas kernels: 39.6 us -> 38.3 us  [on_device(): call(conv_out, cotangent, field_in, kernel, line(ln_gain), line(ln_bias),...]
where the time goes in v6:
time: 41.7 us; the launch traced here: 41.5 us
  Pallas kernels  40.8 us (98%)
  between operations  0.66 us (2%)
    pallas_call x1, Pallas kernels, on_device(): call(conv_out, cotangent, field_in, kernel, line(ln_gain), line(ln_bias),...  38.3 us
    pallas_call x1, Pallas kernels, on_device(): finish(*outs)  2.51 us

profile of v6, /device:TPU:1, one launch (start us, length us, event | category | flops | bytes accessed | tf_op | source)
XLA Modules:
  0.0 41.5 jit_solution(15521351300501061265)
XLA Ops:
  0.6 38.3 %block_backward.1 = (bf16[96,56,128]{2,1,0:T(8,128)(2,1)}, f32[128,512]{1,0:T(8,128)}, f32[512,128]{1,0:T(8,128)}, f32[64,128]{1,0:T(8,128)}) custom-call(bf16[96,56,128]{2,1,0:T(8,128)(2,1)} %x_hbm.1, bf16[96,56,128]{2,1,0:T(8,128)(2,1)} %c_hbm.1, bf16[96,56,128]{2,1,0:T(8,128)(2,1)} %f_hbm.1, f32[49,128]{1,0:T(8,128)} %ker_hbm.1, f32[1,128]{1,0:T(1,128)} %bitcast.14, ...), custom_call_target="tpu_custom_call" | custom-call | flops 6000000000 | bytes 6000000 | tf_op jit(solution)/shard_map/block_backward/pallas_call | solution.py:644
  39.0 2.5 %hand_on.1 = (bf16[96,56,128]{2,1,0:T(8,128)(2,1)}, f32[49,128]{1,0:T(8,128)}, f32[1,128]{1,0:T(1,128)}, f32[1,128]{1,0:T(1,128)}, f32[1,128]{1,0:T(1,128)}, /*i...) custom-call(bf16[96,56,128]{2,1,0:T(8,128)(2,1)} %get-tuple-element., ...), custom_call_target="tpu_custom_call" | custom-call | tf_op jit(solution)/shard_map/hand_on/pallas_call | solution.py:648

commit v7 on v6

--- a/solution.py
+++ b/solution.py
@@ -174,9 +174,6 @@
         mean_two = jnp.concatenate(
             [jnp.concatenate([third, none], 1), jnp.concatenate([none, third], 1)], 0
         )
-        gw[...] = jnp.zeros_like(gw)
-        gbin[...] = jnp.zeros_like(gbin)
-        small[...] = jnp.zeros_like(small)
         acc[...] = jnp.zeros_like(acc)
         kpad[...] = jnp.zeros_like(kpad)
 
@@ -189,7 +186,10 @@
         def cells_of(ref, parts):
             return jnp.concatenate([ref[pl.ds(r0, n), 8 * t : 8 * t + 8, :].astype(f32).reshape(n * 8, CH) for t, r0, n in parts], 0)
 
-        def mlp_grads(parts):
+        def add(ref, at, value, first):
+            ref[at] = value if first else ref[at] + value
+
+        def mlp_grads(parts, first=False):
             value = cells_of(xv, parts)
             center = value - dot(value.astype(bf16), third)
             rstd = lax.rsqrt(dot((center * center).astype(bf16), third) + EPS)
@@ -213,13 +213,13 @@
                 acts.append((h * above).astype(bf16))
                 dpres.append(d_pre.astype(bf16))
             act, d_pre = jnp.concatenate(acts, 0), jnp.concatenate(dpres, 0)
-            gbin[...] += g_bin
-            gw[CH:, :] += dot_rows(cb, act)
-            gw[:CH, :] += dot_rows(zed, d_pre)
-            small[3] += rows8(cot)
+            add(gbin, ..., g_bin, first)
+            add(gw, slice(CH, 2 * CH), dot_rows(cb, act), first)
+            add(gw, slice(0, CH), dot_rows(zed, d_pre), first)
+            add(small, 3, rows8(cot), first)
             return d_pre, normed, rstd
 
-        def mlp_du(parts, d_pre, normed, rstd):
+        def mlp_du(parts, d_pre, normed, rstd, first=False):
             d_zed = dot_last(d_pre, win_ref[...])
             d_gain = d_zed * normed
             d_norm = d_zed * gain
@@ -231,13 +231,12 @@
             for t, r0, n in parts:
                 dup[pl.ds(3 + r0, n), 4 + 8 * t : 12 + 8 * t, :] = du[at : at + 8 * n].reshape(n, 8, CH)
                 at += 8 * n
-            small[0] += rows8(d_gain)
-            small[1] += rows8(d_zed)
-            small[2] += rows8(du)
+            for q, value in enumerate((d_gain, d_zed, du)):
+                add(small, q, rows8(value), first)
 
         for i in range(4):
             load(i).wait()
-        mlp_du(RIM, *mlp_grads(RIM))
+        mlp_du(RIM, *mlp_grads(RIM, True), first=True)
 
         half = LAT_ROWS // 2
         low = lax.broadcasted_iota(jnp.int32, (half, 8, CH), 1) < 4
@@ -571,7 +570,7 @@
 ]
 HANDED = [RESULTS[0], RESULTS[5], RESULTS[7], jax.ShapeDtypeStruct((SMALL, CH), f32)]
 ROWS = ((2, 55), (3, 53), (4, 54), (8, 56), (9, 57))
-BANDS = 4
+BANDS = 2
 
 
 def hand_on(*refs):

time: 41.7 us -> 41.7 us (level)
  no operation moved by 1% of the time
where the time goes in v7:
time: 41.7 us; the launch traced here: 41.6 us
  Pallas kernels  40.9 us (98%)
  between operations  0.66 us (2%)
    pallas_call x1, Pallas kernels, on_device(): call(conv_out, cotangent, field_in, kernel, line(ln_gain), line(ln_bias),...  38.3 us
    pallas_call x1, Pallas kernels, on_device(): finish(*outs)  2.59 us

profile of v7, /device:TPU:1, one launch (start us, length us, event | category | flops | bytes accessed | tf_op | source)
XLA Modules:
  0.0 41.6 jit_solution(8381354725274197036)
XLA Ops:
  0.6 38.3 %block_backward.1 = (bf16[96,56,128]{2,1,0:T(8,128)(2,1)}, f32[128,512]{1,0:T(8,128)}, f32[512,128]{1,0:T(8,128)}, f32[64,128]{1,0:T(8,128)}) custom-call(bf16[96,56,128]{2,1,0:T(8,128)(2,1)} %x_hbm.1, bf16[96,56,128]{2,1,0:T(8,128)(2,1)} %c_hbm.1, bf16[96,56,128]{2,1,0:T(8,128)(2,1)} %f_hbm.1, f32[49,128]{1,0:T(8,128)} %ker_hbm.1, f32[1,128]{1,0:T(1,128)} %bitcast.14, ...), custom_call_target="tpu_custom_call" | custom-call | flops 6000000000 | bytes 6000000 | tf_op jit(solution)/shard_map/block_backward/pallas_call | solution.py:643
  39.0 2.6 %hand_on.1 = (bf16[96,56,128]{2,1,0:T(8,128)(2,1)}, f32[49,128]{1,0:T(8,128)}, f32[1,128]{1,0:T(1,128)}, f32[1,128]{1,0:T(1,128)}, f32[1,128]{1,0:T(1,128)}, /*i...) custom-call(bf16[96,56,128]{2,1,0:T(8,128)(2,1)} %get-tuple-element., ...), custom_call_target="tpu_custom_call" | custom-call | tf_op jit(solution)/shard_map/hand_on/pallas_call | solution.py:647
